TPU v7x, 32 devices: a whole 2x2x4 slice. The times are simulated.
32 devices in a mesh: rep: 4 (over z), shard: 8 (over y, x, core).
Axes of the slice: x: 2, y: 2, z: 4, core: 2. Of those that a mesh axis runs over, the one named last changes fastest.
Arguments:
- tokens: bfloat16 [16384, 768], P(('rep', 'shard')), may hold values from -6 to 6
- cotangent: bfloat16 [16384, 768], P(('rep', 'shard')), may hold values from -6 to 6
- segments: int32 [16384], P(('rep', 'shard')), may hold values from 0 to 31, never falling along the last dimension, each value on 1 to 1024 neighbouring positions
- buckets: int32 [512], replicated, may hold values from 0 to 31, as said below
- routes: int32 [16384, 2], P(('rep', 'shard')), may hold values from 0 to 7, all different within a row; in each aligned block of 512 rows (0 to 511, 512 to 1023, ...) at most 224 rows name the same one
- attn_gain: bfloat16 [768], P('shard'), may hold values from 0.5 to 1.5
- qkv_weight: bfloat16 [768, 2304], P('shard'), may hold values from -0.21875 to 0.21875
- proj_weight: bfloat16 [768, 768], P('shard'), may hold values from -1.25 to 1.25
- rel_bias: float32 [32, 12], replicated, may hold values from -4 to 4
- moe_gain: bfloat16 [768], P('shard'), may hold values from 0.5 to 1.5
- router: bfloat16 [768, 8], P('shard'), may hold values from -0.15625 to 0.15625
- expert_in: bfloat16 [8, 768, 3072], P('shard'), may hold values from -0.21875 to 0.21875
- expert_out: bfloat16 [8, 3072, 768], P('shard'), may hold values from -0.21875 to 0.21875
Outputs:
- output: bfloat16 [16384, 768], P(('rep', 'shard'))
- grad_tokens: bfloat16 [16384, 768], P(('rep', 'shard'))
- grad_qkv: float32 [768, 2304], P('shard')
- grad_proj: float32 [768, 768], P('shard')
- grad_router: float32 [768, 8], P('shard')
- grad_attn_gain: float32 [768], P('shard')
- grad_moe_gain: float32 [768], P('shard')
- grad_rel_bias: float32 [32, 12], replicated
- grad_expert_in: float32 [8, 768, 3072], P('shard', 'rep')
- grad_expert_out: float32 [8, 3072, 768], P('shard', 'rep')
Inputs may be any that keep to these rules, and one draw needn't show every extreme that they name: `segments`: never falling along the tokens; one number covers at most 1024 tokens, and some number exactly that many. `buckets`: never falling with the distance, 0 at distance 0. `routes`: a token's 2 experts differ; the 512 tokens of one device name one expert at most 224 times, and some device's tokens name some expert exactly 224 times.
All inputs are finite; a program needn't handle non-finite values.
Results may differ from a plain program's by a relative error of at most 0.017.
Values may be sent and summed in bfloat16 or wider, within the bound.
No kernel may reach another device: no remote copies, remote signals or barrier semaphores. Data moves between devices by JAX's collectives and lax.ppermute only.
A program may use at most 192 MiB of HBM per device.

v0:
```python
import jax
import jax.numpy as jnp
from jax import lax
from jax.sharding import PartitionSpec as P

epsilon = 1e-06
neg_fill = -1e30


def rms_norm(values, gain_vector):
    return (
        values
        * lax.rsqrt(jnp.mean(values * values, axis=-1, keepdims=True) + epsilon)
        * gain_vector
    )


def gelu_exact(values):
    return jax.nn.gelu(values, approximate=False)


def toeplitz_rows(series):
    lead = series.shape[:-1]
    length = series.shape[-1]
    widened = jnp.concatenate([series[..., ::-1], jnp.zeros_like(series)], axis=-1)
    tiled = jnp.broadcast_to(widened[..., None, :], lead + (length, 2 * length))
    flattened = tiled.reshape(lead + (length * 2 * length,))[..., : length * (2 * length - 1)]
    return flattened.reshape(lead + (length, 2 * length - 1))[..., length - 1 :]


def block_scores(query_rows, keys_low, bias_rows, segment_rows, segments, row_start, score_scale):
    row_count = query_rows.shape[0]
    key_count = keys_low.shape[0]
    raw_scores = jnp.einsum(
        "rhd,khd->hrk", query_rows, keys_low, preferred_element_type=jnp.float32
    )
    offset = (
        row_start
        + lax.broadcasted_iota(jnp.int32, (row_count, key_count), 0)
        - lax.broadcasted_iota(jnp.int32, (row_count, key_count), 1)
    )
    scores = raw_scores * score_scale + bias_rows
    allowed = (offset >= 0) & (segment_rows[:, None] == segments[None, :])
    return jnp.where(allowed[None], scores, neg_fill)


def expert_forward(expert_rows, expert_in, expert_out):
    pre_act = jnp.einsum("erd,edf->erf", expert_rows, expert_in, preferred_element_type=jnp.float32)
    activated, gelu_back = jax.vjp(gelu_exact, pre_act)
    act_low = activated.astype(jnp.bfloat16)
    expert_result = jnp.einsum(
        "erf,efd->erd", act_low, expert_out, preferred_element_type=jnp.float32
    ).astype(jnp.bfloat16)
    return (act_low, gelu_back, expert_result)


def expert_backward(expert_rows, act_low, gelu_back, grad_rows, expert_in, expert_out):
    grad_act = jnp.einsum("erd,efd->erf", grad_rows, expert_out, preferred_element_type=jnp.float32)
    grad_expert_out = jnp.einsum(
        "erf,erd->efd", act_low, grad_rows, preferred_element_type=jnp.float32
    )
    grad_pre = gelu_back(grad_act)[0].astype(jnp.bfloat16)
    grad_expert_in = jnp.einsum(
        "erd,erf->edf", expert_rows, grad_pre, preferred_element_type=jnp.float32
    )
    grad_sent = jnp.einsum(
        "erf,edf->erd", grad_pre, expert_in, preferred_element_type=jnp.float32
    ).astype(jnp.bfloat16)
    return (grad_expert_in, grad_expert_out, grad_sent)


def body(
    tokens,
    cotangent,
    segments,
    buckets,
    routes,
    attn_gain,
    qkv_weight,
    proj_weight,
    rel_bias,
    moe_gain,
    router,
    expert_in,
    expert_out,
):
    seq_len, model_width = tokens.shape
    head_count = rel_bias.shape[1]
    bucket_count = rel_bias.shape[0]
    head_dim = model_width // head_count
    top_count = routes.shape[1]
    local_experts = expert_in.shape[0]
    experts_all = local_experts * lax.axis_size("shard")
    capacity = 3 * seq_len * top_count // (2 * experts_all)
    score_scale = head_dim ** (-0.5)
    block_rows = 512
    block_count = seq_len // block_rows
    gain_full, qkv_full, proj_full, moe_gain_full, router_full = (
        lax.all_gather(attn_gain, "shard", axis=0, tiled=True),
        lax.all_gather(qkv_weight, "shard", axis=0, tiled=True),
        lax.all_gather(proj_weight, "shard", axis=0, tiled=True),
        lax.all_gather(moe_gain, "shard", axis=0, tiled=True),
        lax.all_gather(router, "shard", axis=0, tiled=True),
    )
    inputs = tokens.astype(jnp.float32)
    normed_one, norm_one_back = jax.vjp(rms_norm, inputs, gain_full.astype(jnp.float32))
    normed_low = normed_one.astype(jnp.bfloat16)
    projected = jnp.dot(normed_low, qkv_full, preferred_element_type=jnp.float32).astype(
        jnp.bfloat16
    )
    queries = projected[:, :model_width].reshape(seq_len, head_count, head_dim)
    keys_low = projected[:, model_width : 2 * model_width].reshape(seq_len, head_count, head_dim)
    values_low = projected[:, 2 * model_width :].reshape(seq_len, head_count, head_dim)
    bucket_hot = (buckets[:, None] == jnp.arange(bucket_count)[None, :]).astype(jnp.float32)
    dist_bias = jnp.einsum("sb,bh->hs", bucket_hot, rel_bias, precision=lax.Precision.HIGHEST)
    bias_table = toeplitz_rows(dist_bias)
    bucket_grid = toeplitz_rows(buckets)
    grid_hot = (bucket_grid[:, :, None] == jnp.arange(bucket_count)[None, None, :]).astype(
        jnp.bfloat16
    )

    def forward_block(block_index):
        row_start = block_index * block_rows
        scores = block_scores(
            queries, keys_low, bias_table, segments, segments, row_start, score_scale
        )
        row_top = jnp.max(scores, axis=-1, keepdims=True)
        weights = jnp.exp(scores - row_top)
        row_total = jnp.sum(weights, axis=-1, keepdims=True)
        weights_low = (weights / row_total).astype(jnp.bfloat16)
        mixed_rows = jnp.einsum(
            "hrk,khd->rhd", weights_low, values_low, preferred_element_type=jnp.float32
        )
        return (mixed_rows.astype(jnp.bfloat16), (row_top + jnp.log(row_total))[:, :, 0])

    attended, log_totals = lax.map(forward_block, jnp.arange(block_count))
    attended = attended.reshape(seq_len, model_width)
    residual = inputs + jnp.dot(attended, proj_full, preferred_element_type=jnp.float32)
    normed_two, norm_two_back = jax.vjp(rms_norm, residual, moe_gain_full.astype(jnp.float32))
    moe_low = normed_two.astype(jnp.bfloat16)
    logits = jnp.dot(moe_low, router_full, preferred_element_type=jnp.float32)
    pair_expert = routes.reshape(-1)
    matches = pair_expert[:, None] == jnp.arange(experts_all)[None, :]
    match_count = matches.astype(jnp.int32)
    slot_rank = jnp.sum((jnp.cumsum(match_count, axis=0) - match_count) * match_count, axis=1)
    kept = slot_rank < capacity
    kept_scale = kept.astype(jnp.float32).reshape(seq_len, top_count, 1)
    flat_slot = jnp.where(kept, pair_expert * capacity + slot_rank, 0)
    slot_match = (flat_slot[None, :] == jnp.arange(experts_all * capacity)[:, None]) & kept[None, :]
    slot_pair = jnp.max(jnp.where(slot_match, jnp.arange(seq_len * top_count)[None, :], -1), axis=1)
    slot_used = (slot_pair >= 0)[:, None]
    pair_index = jnp.maximum(slot_pair, 0)
    sent = jnp.where(
        slot_used, jnp.take(moe_low, pair_index // top_count, axis=0), jnp.zeros((), jnp.bfloat16)
    )
    sent = sent.reshape(experts_all, capacity, model_width)
    route_hot = matches.reshape(seq_len, top_count, experts_all).astype(jnp.float32)
    chosen = jnp.sum(route_hot * logits[:, None, :], axis=2)
    gate_weights = jax.nn.softmax(chosen, axis=1)
    grad_out = cotangent.astype(jnp.float32)
    pair_grads = (
        (gate_weights[:, :, None] * grad_out[:, None, :])
        .astype(jnp.bfloat16)
        .reshape(seq_len * top_count, model_width)
    )
    slot_grads = jnp.where(
        slot_used, jnp.take(pair_grads, pair_index, axis=0), jnp.zeros((), jnp.bfloat16)
    )
    slot_grads = slot_grads.reshape(experts_all, capacity, model_width)
    expert_rows = lax.all_to_all(sent, "shard", split_axis=0, concat_axis=1, tiled=True)
    act_low, gelu_back, expert_result = expert_forward(expert_rows, expert_in, expert_out)
    returned = lax.all_to_all(expert_result, "shard", split_axis=1, concat_axis=0, tiled=True)
    grad_rows = lax.all_to_all(slot_grads, "shard", split_axis=0, concat_axis=1, tiled=True)
    grad_expert_in, grad_expert_out, grad_sent = expert_backward(
        expert_rows, act_low, gelu_back, grad_rows, expert_in, expert_out
    )
    grad_back = lax.all_to_all(grad_sent, "shard", split_axis=1, concat_axis=0, tiled=True)
    returned = returned.reshape(experts_all * capacity, model_width)
    picked = (
        jnp.take(returned, flat_slot, axis=0)
        .reshape(seq_len, top_count, model_width)
        .astype(jnp.float32)
        * kept_scale
    )
    output = residual + jnp.sum(gate_weights[:, :, None] * picked, axis=1)
    grad_gates = jnp.sum(grad_out[:, None, :] * picked, axis=2)
    grad_back = grad_back.reshape(experts_all * capacity, model_width)
    grad_normed_two = jnp.sum(
        jnp.take(grad_back, flat_slot, axis=0)
        .reshape(seq_len, top_count, model_width)
        .astype(jnp.float32)
        * kept_scale,
        axis=1,
    )
    grad_chosen = gate_weights * (
        grad_gates - jnp.sum(gate_weights * grad_gates, axis=1, keepdims=True)
    )
    grad_logits = jnp.sum(grad_chosen[:, :, None] * route_hot, axis=1).astype(jnp.bfloat16)
    grad_router = jnp.einsum("td,te->de", moe_low, grad_logits, preferred_element_type=jnp.float32)
    grad_normed_two = grad_normed_two + jnp.einsum(
        "te,de->td", grad_logits, router_full, preferred_element_type=jnp.float32
    )
    grad_residual, grad_moe_gain = norm_two_back(grad_normed_two)
    grad_residual = grad_residual + grad_out
    grad_branch = grad_residual.astype(jnp.bfloat16)
    grad_proj = jnp.einsum("td,te->de", attended, grad_branch, preferred_element_type=jnp.float32)
    grad_attended = jnp.einsum(
        "te,de->td", grad_branch, proj_full, preferred_element_type=jnp.float32
    ).astype(jnp.bfloat16)
    grad_attended = grad_attended.reshape(seq_len, head_count, head_dim)

    def backward_block(carry, block_index):
        grad_keys, grad_values, bucket_grad = carry
        row_start = block_index * block_rows
        row_log = log_totals[block_index]
        scores = block_scores(
            queries, keys_low, bias_table, segments, segments, row_start, score_scale
        )
        weights = jnp.exp(scores - row_log[:, :, None])
        grad_weights = jnp.einsum(
            "rhd,khd->hrk", grad_attended, values_low, preferred_element_type=jnp.float32
        )
        row_dot = jnp.sum(weights * grad_weights, axis=-1, keepdims=True)
        grad_scores = (weights * (grad_weights - row_dot)).astype(jnp.bfloat16)
        grad_queries = (
            jnp.einsum("hrk,khd->rhd", grad_scores, keys_low, preferred_element_type=jnp.float32)
            * score_scale
        )
        grad_keys = (
            grad_keys
            + jnp.einsum("hrk,rhd->khd", grad_scores, queries, preferred_element_type=jnp.float32)
            * score_scale
        )
        grad_values = grad_values + jnp.einsum(
            "hrk,rhd->khd",
            weights.astype(jnp.bfloat16),
            grad_attended,
            preferred_element_type=jnp.float32,
        )
        bucket_grad = bucket_grad + jnp.einsum(
            "hrk,rkb->bh", grad_scores, grid_hot, preferred_element_type=jnp.float32
        )
        return ((grad_keys, grad_values, bucket_grad), grad_queries)

    zero_heads = jnp.zeros((seq_len, head_count, head_dim), jnp.float32)
    zero_bucket = jnp.zeros((bucket_count, head_count), jnp.float32)
    (grad_keys, grad_values, grad_rel_bias), grad_queries = lax.scan(
        backward_block, (zero_heads, zero_heads, zero_bucket), jnp.arange(block_count)
    )
    grad_projected = jnp.concatenate(
        [
            grad_queries.reshape(seq_len, model_width),
            grad_keys.reshape(seq_len, model_width),
            grad_values.reshape(seq_len, model_width),
        ],
        axis=1,
    ).astype(jnp.bfloat16)
    grad_qkv = jnp.einsum(
        "td,te->de", normed_low, grad_projected, preferred_element_type=jnp.float32
    )
    grad_normed_one = jnp.einsum(
        "te,de->td", grad_projected, qkv_full, preferred_element_type=jnp.float32
    )
    grad_inputs, grad_attn_gain = norm_one_back(grad_normed_one)
    grad_tokens = (grad_inputs + grad_residual).astype(jnp.bfloat16)
    grad_expert_in, grad_expert_out = (
        lax.psum_scatter(
            grad_expert_in.astype(jnp.bfloat16), "rep", scatter_dimension=1, tiled=True
        ).astype(jnp.float32),
        lax.psum_scatter(
            grad_expert_out.astype(jnp.bfloat16), "rep", scatter_dimension=1, tiled=True
        ).astype(jnp.float32),
    )
    owned_attn, owned_qkv, owned_proj, owned_moe, owned_router = (
        lax.psum_scatter(grad_attn_gain, "shard", scatter_dimension=0, tiled=True),
        lax.psum_scatter(grad_qkv, "shard", scatter_dimension=0, tiled=True),
        lax.psum_scatter(grad_proj, "shard", scatter_dimension=0, tiled=True),
        lax.psum_scatter(grad_moe_gain, "shard", scatter_dimension=0, tiled=True),
        lax.psum_scatter(grad_router, "shard", scatter_dimension=0, tiled=True),
    )
    owned_attn, owned_qkv, owned_proj, owned_moe, owned_router = (
        lax.psum(owned_attn.astype(jnp.bfloat16), "rep").astype(jnp.float32),
        lax.psum(owned_qkv.astype(jnp.bfloat16), "rep").astype(jnp.float32),
        lax.psum(owned_proj.astype(jnp.bfloat16), "rep").astype(jnp.float32),
        lax.psum(owned_moe.astype(jnp.bfloat16), "rep").astype(jnp.float32),
        lax.psum(owned_router.astype(jnp.bfloat16), "rep").astype(jnp.float32),
    )
    grad_rel_bias = lax.psum(grad_rel_bias, ("rep", "shard"))
    return (
        output.astype(jnp.bfloat16),
        grad_tokens,
        owned_qkv,
        owned_proj,
        owned_router,
        owned_attn,
        owned_moe,
        grad_rel_bias,
        grad_expert_in,
        grad_expert_out,
    )


def solution(mesh):
    return jax.shard_map(
        body,
        mesh=mesh,
        in_specs=(
            P(("rep", "shard"), None),
            P(("rep", "shard"), None),
            P(("rep", "shard")),
            P(),
            P(("rep", "shard"), None),
            P("shard"),
            P("shard", None),
            P("shard", None),
            P(),
            P("shard"),
            P("shard", None),
            P("shard", None, None),
            P("shard", None, None),
        ),
        out_specs=(
            P(("rep", "shard"), None),
            P(("rep", "shard"), None),
            P("shard", None),
            P("shard", None),
            P("shard", None),
            P("shard"),
            P("shard"),
            P(),
            P("shard", "rep", None),
            P("shard", "rep", None),
        ),
        check_vma=False,
    )
```

profile of v0, /device:TPU:4, one launch (start us, length us, event | category | flops | bytes accessed | tf_op | source)
XLA Modules:
  0.0 1014.2 jit_solution(11014900650223688416)
XLA Ops:
  9.9 2.3 reduce-window.6
  20.5 12.9 %all-reduce.7 = (bf16[768]{0:T(1024)(128)(2,1)S(1)}, bf16[768]{0:T(1024)(128)(2,1)S(1)}) all-reduce(bf16[768]{0:T(1024)(128)(2,1)S(1)} %dynamic-update-slice, bf16[768]{0:T(1024)(128)(2,1)S(1)} %dynamic-update-slice.1), channel_id=1, replica_groups=mesh['rep'=4,'shard'=8] {'shard'}, use_global_device_ids=true, to_apply=%add.2 | all-reduce | flops 1536 | bytes 6144
  36.6 11.7 %broadcast_in_dim.159 = f32[12,512,1024]{2,1,0:T(8,128)} broadcast(f32[12,1024]{1,0:T(8,128)S(1)} %concatenate.10), dimensions={0,2} | broadcast | bytes 25214976 | tf_op jit(solution)/shard_map/broadcast_in_dim | solution.py:26
  48.3 11.0 %pad.9 = f32[16,512,1024]{2,1,0:T(8,128)S(1)} pad(f32[12,512,1024]{2,1,0:T(8,128)} %broadcast_in_dim.159, f32[]{:T(128)} %constant.59.clone.1), padding=0_4x0_0x0_0 | pad | bytes 58720260
  59.2 39.7 %copy.119 = f32[2,8,512,1024]{3,1,2,0:T(8,128)} copy(f32[2,8,512,1024]{3,2,1,0:T(8,128)S(1)} %bitcast.131) | data formatting | bytes 67108864
  98.9 22.6 %slice.47 = f32[12,523776]{1,0:T(8,128)} slice(f32[12,524288]{1,0:T(8,128)} %bitcast.132), slice={[0:12], [0:523776]} | slice | bytes 50282496 | tf_op jit(solution)/shard_map/slice | solution.py:27
  121.5 54.0 %reshape.558 = f32[12,512,1023]{2,1,0:T(8,128)} reshape(f32[12,523776]{1,0:T(8,128)} %slice.47) | data formatting | bytes 50282496 | tf_op jit(solution)/shard_map/reshape | solution.py:28
  175.5 13.4 %slice.48 = f32[12,512,512]{2,1,0:T(8,128)} slice(f32[12,512,1023]{2,1,0:T(8,128)} %reshape.558), slice={[0:12], [0:512], [511:1023]} | slice | bytes 25165824 | tf_op jit(solution)/shard_map/slice | solution.py:28
  188.9 12.6 %copy.118 = f32[12,512,512]{1,2,0:T(8,128)} copy(f32[12,512,512]{2,1,0:T(8,128)} %slice.48) | data formatting | bytes 25165824
  201.9 4.1 convolution_convert_fusion.2
  209.4 6.6 fusion.83
  217.9 2.6 copy-done.4
  220.7 2.5 fusion.49
  223.3 2.5 multiply_reduce_fusion.6
  227.2 5.0 gather_fusion
  232.9 32.2 %all_to_all.16 = bf16[8,192,768]{2,1,0:T(8,128)(2,1)S(1)} all-to-all(bf16[8,192,768]{2,1,0:T(8,128)(2,1)S(1)} %select_select_fusion.1), channel_id=1, replica_groups=mesh['rep'=4,'shard'=8] {'shard'}, dimensions={0} | all-to-all | bytes 4718592 | tf_op jit(solution)/shard_map/all_to_all | solution.py:170
  265.0 49.3 %multiply_convert_fusion = (bf16[1536,3072]{1,0:T(8,128)(2,1)S(1)}, f32[1536,3072]{1,0:T(8,128)}, f32[1536,3072]{1,0:T(8,128)}) fusion(bf16[1536,768]{1,0:T(8,128)(2,1)S(1)} %bitcast.152, bf16[1,768,3072]{2,1,0:T(8,128)(2,1)S(1)} %bitcast.167), kind=kOutput, calls=%fused_computation.9 | convolution fusion | flops 7554465792 | bytes 54263808 | tf_op jit(solution)/shard_map/erd,edf->erf/dot_general | solution.py:48
  314.4 7.7 fusion.31
  322.1 33.8 %copy.134 = bf16[1,1536,768]{2,0,1:T(2,128)(2,1)} copy(bf16[1,1536,768]{2,1,0:T(8,128)(2,1)S(1)} %fusion.31) | data formatting | bytes 4718592 | tf_op jit(solution)/shard_map/convert_element_type | solution.py:53
  356.4 24.1 %reduce.5 = bf16[1536,768]{1,0:T(8,128)(2,1)S(1)} reduce(bf16[1536,1,768]{2,1,0:T(2,128)(2,1)} %bitcast.135, bf16[]{:T(256)} %broadcast.521), dimensions={1}, to_apply=%bitcast.126.reduce_sub_computation | reduce | bytes 4718594
  380.5 3.3 reshape.650
  383.8 5.0 all-to-all-start.1
  388.8 31.1 %all-gather = bf16[8,96,8]{1,2,0:T(8,128)(2,1)S(1)} all-gather(bf16[1,96,8]{1,2,0:T(8,128)(2,1)S(1)} %bitcast.163), channel_id=1, replica_groups=mesh['rep'=4,'shard'=8] {'shard'}, dimensions={0}, use_global_device_ids=true | all-gather | bytes 13824 | tf_op jit(solution)/shard_map/all_gather | solution.py:103
  420.1 3.6 mul.286
  423.7 5.2 mul.287
  429.5 4.7 reshape.651
  434.2 2.7 copy.132
  436.9 5.2 gather_fusion.2
  442.1 3.2 multiply_reduce_fusion.1
  448.2 5.6 gather_fusion.1
  455.9 32.3 %all_to_all.17 = bf16[8,192,768]{2,1,0:T(8,128)(2,1)S(1)} all-to-all(bf16[8,192,768]{2,1,0:T(8,128)(2,1)S(1)} %select_select_fusion), channel_id=1, replica_groups=mesh['rep'=4,'shard'=8] {'shard'}, dimensions={0} | all-to-all | bytes 4718592 | tf_op jit(solution)/shard_map/all_to_all | solution.py:173
  488.3 22.5 %add_convert_fusion = bf16[1536,3072]{1,0:T(8,128)(2,1)} fusion(f32[1536,3072]{1,0:T(8,128)} %get-tuple-element.92, f32[1536,3072]{1,0:T(8,128)} %get-tuple-element.115, bf16[1536,768]{1,0:T(8,128)(2,1)S(1)} %bitcast.154, bf16[1,3072,768]{2,1,0:T(8,128)(2,1)S(1)} %bitcast.165), kind=kOutput, calls=%fused_computation.8 | convolution fusion | flops 7313817600 | bytes 54263808 | tf_op jit(solution)/shard_map/erd,efd->erf/dot_general | solution.py:58
  510.8 11.5 %fusion.34 = bf16[1,1536,768]{2,1,0:T(8,128)(2,1)S(1)} fusion(bf16[1536,3072]{1,0:T(8,128)(2,1)} %add_convert_fusion, bf16[1,768,3072]{2,1,0:T(8,128)(2,1)} %param.26), kind=kOutput, calls=%fused_computation.63 | convolution fusion | flops 7248936960 | bytes 16515072 | tf_op jit(solution)/shard_map/erf,edf->erd/dot_general | solution.py:66
  522.3 33.7 %copy.133 = bf16[1,1536,768]{2,0,1:T(2,128)(2,1)} copy(bf16[1,1536,768]{2,1,0:T(8,128)(2,1)S(1)} %fusion.34) | data formatting | bytes 4718592 | tf_op jit(solution)/shard_map/convert_element_type | solution.py:68
  556.0 24.3 %reduce.6 = bf16[1536,768]{1,0:T(8,128)(2,1)S(1)} reduce(bf16[1536,1,768]{2,1,0:T(2,128)(2,1)} %bitcast.136, bf16[]{:T(256)} %broadcast.521), dimensions={1}, to_apply=%bitcast.125.reduce_sub_computation | reduce | bytes 4718594
  580.4 3.3 reshape.648
  583.6 5.0 all-to-all-start.3
  590.8 26.8 %all-to-all-done.3 = bf16[8,2,73728]{2,1,0:T(2,128)(2,1)S(1)} async-done(((bf16[8,2,73728]{2,1,0:T(2,128)(2,1)}), bf16[8,2,73728]{2,1,0:T(2,128)(2,1)S(1)}, u32[]{:S(2)}, u32[]{:S(2)}) %all-to-all-start.3) | async-done | bytes 2359328 | tf_op jit(solution)/shard_map/all_to_all | solution.py:177
  617.7 4.6 reshape.649
  622.2 2.7 copy.131
  625.0 5.2 gather_fusion.3
  630.2 4.9 select_convert_fusion.1
  635.1 3.7 reshape.573
  638.9 5.2 reshape.575
  644.1 18.1 %multiply_reduce_fusion.2 = (f32[512,768]{1,0:T(8,128)S(1)}, f32[512,768]{1,0:T(8,128)S(1)}) fusion(f32[512,2,768]{2,1,0:T(2,128)} %reshape.575, f32[512,2]{1,0:T(8,128)} %reshape.574, f32[512,2,768]{2,1,0:T(2,128)S(1)} %reshape.573, f32[512,2]{1,0:T(8,128)S(1)} %copy.96), kind=kLoop, calls=%fused_computation.54 | loop fusion | flops 3145728 | bytes 9445376 | tf_op jit(solution)/shard_map/reduce_sum | solution.py:188
  666.9 3.0 convolution_convert_fusion.3
  671.5 10.8 %multiply_reduce_fusion = (f32[12,512]{1,0:T(8,128)S(1)}, f32[12,512,512]{1,2,0:T(8,128)}) fusion(f32[12,512,512]{1,2,0:T(8,128)} %copy-done.4, f32[12,512]{1,0:T(8,128)S(1)} %log_add_fusion, bf16[512,12,64]{0,2,1:T(8,128)(2,1)S(1)} %bitcast.144, bf16[512,12,64]{0,2,1:T(8,128)(2,1)S(1)} %bitcast.149), kind=kOutput, calls=%fused_computation.25 | convolution fusion | flops 412084224 | bytes 26787840 | tf_op jit(solution)/shard_map/while/body/eval_jaxpr/rhd,khd->hrk/dot_general | solution.py:220
  684.5 7.0 multiply_convert_fusion.1
  699.3 5.2 fusion.54
  704.6 12.8 %fusion.24 = bf16[1,3072,768]{2,1,0:T(8,128)(2,1)} fusion(bf16[1536,3072]{1,0:T(8,128)(2,1)} %copy-done.54, bf16[1536,768]{1,0:T(8,128)(2,1)} %bitcast.155), kind=kOutput, calls=%fused_computation.49 | convolution fusion | flops 7250116608 | bytes 16515072 | tf_op jit(solution)/shard_map/erf,erd->efd/dot_general | solution.py:59
  717.4 12.4 %fusion.23 = bf16[1,768,3072]{2,1,0:T(8,128)(2,1)} fusion(bf16[1536,768]{1,0:T(8,128)(2,1)} %bitcast.153, bf16[1536,3072]{1,0:T(8,128)(2,1)} %add_convert_fusion), kind=kOutput, calls=%fused_computation.48 | convolution fusion | flops 7250116608 | bytes 16515072 | tf_op jit(solution)/shard_map/erd,erf->edf/dot_general | solution.py:63
  732.6 4.4 reshape.572
  741.5 12.5 %fusion.50 = f32[32,12]{0,1:T(8,128)S(1)} fusion(bf16[12,512,512]{1,2,0:T(8,128)(2,1)} %copy-done.5, s32[512,512]{0,1:T(8,128)} %copy.108), kind=kOutput, calls=%fused_computation.94 | convolution fusion | flops 209715200 | bytes 7341568 | tf_op jit(solution)/shard_map/while/body/eval_jaxpr/hrk,rkb->bh/dot_general | solution.py:240
  755.6 27.9 %reduce-scatter.8.cloned.1.call-done = f32[96,2304]{1,0:T(8,128)} async-done(((f32[768,2304]{1,0:T(8,128)}), f32[96,2304]{1,0:T(8,128)}) %reduce-scatter.8.cloned.1.call-update) | async-done | bytes 884752 | tf_op jit(solution)/shard_map/reduce_scatter | solution.py:276
  785.6 5.9 fusion.40
  791.5 13.7 %all-reduce.6 = (bf16[768]{0:T(1024)(128)(2,1)S(1)}, bf16[768]{0:T(1024)(128)(2,1)S(1)}) all-reduce(f32[768]{0:T(1024)S(1)} %get-tuple-element.63, f32[768]{0:T(1024)S(1)} %get-tuple-element.61), channel_id=5, replica_groups=mesh['rep'=4,'shard'=8] {'shard'}, use_global_device_ids=true, to_apply=%region_26.28.clone | all-reduce | flops 1536 | bytes 9216
  805.4 11.9 %all-reduce.8 = (bf16[96,8]{0,1:T(8,128)(2,1)S(1)}, bf16[96]{0:T(256)(128)(2,1)S(1)}, bf16[96]{0:T(256)(128)(2,1)S(1)}) all-reduce(bf16[96,8]{0,1:T(8,128)(2,1)S(1)} %copy.115, bf16[96]{0:T(256)(128)(2,1)S(1)} %dynamic-slice.9, bf16[96]{0:T(256)(128)(2,1)S(1)} %dynamic-slice.8), channel_id=1, replica_groups=mesh['rep'=4,'shard'=8] {'rep'}, use_global_device_ids=true, to_apply=%region_24.26 | all-reduce | flops 960 | bytes 3840 | tf_op jit(solution)/shard_map/psum | solution.py:286
  818.9 44.1 %psum.47 = f32[32,12]{0,1:T(8,128)} all-reduce(f32[32,12]{0,1:T(8,128)S(1)} %fusion.50), channel_id=1, replica_groups=mesh['rep'=4,'shard'=8] {'rep','shard'}, use_global_device_ids=true, to_apply=%region_31.33 | all-reduce | flops 384 | bytes 3072 | tf_op jit(solution)/shard_map/psum | solution.py:288
  863.0 2.8 fusion.43
  865.8 6.7 reduce-scatter.14.cloned.1.call-done
  872.4 2.8 convert_element_type.215
  875.3 85.1 %reduce-scatter.12.cloned.1.call-done = bf16[1,192,3072]{2,1,0:T(8,128)(2,1)} async-done(((bf16[1,768,3072]{2,1,0:T(8,128)(2,1)}), bf16[1,192,3072]{2,1,0:T(8,128)(2,1)}) %reduce-scatter.12.cloned.1.call-update) | async-done | bytes 1179664 | tf_op jit(solution)/shard_map/reduce_scatter | solution.py:267
  960.4 2.9 convert_element_type.212
  963.3 40.2 %all-reduce.12.cloned.1.call-done = (bf16[96,2304]{1,0:T(8,128)(2,1)}, bf16[96,768]{1,0:T(8,128)(2,1)}) async-done(((bf16[96,2304]{1,0:T(8,128)(2,1)}, bf16[96,768]{1,0:T(8,128)(2,1)}), (bf16[96,2304]{1,0:T(8,128)(2,1)}, bf16[96,768]{1,0:T(8,128)(2,1)})) %all-reduce.12.cloned.1.call-update) | async-done | bytes 589840 | tf_op jit(solution)/shard_map/psum | solution.py:283
  (234 shorter events, 61.6 us)
Async XLA Ops:
  7.2 28.1 %copy-start = (f32[32,12]{0,1:T(8,128)S(1)}, f32[32,12]{0,1:T(8,128)}, u32[]{:S(2)}) copy-start(f32[32,12]{0,1:T(8,128)} %param.23) | copy-start | bytes 4612
  7.2 194.7 %all-gather.4.cloned.1.call-start = ((), (), s32[]{:S(2)}) async-start(), calls=%async_computation.9 | async-start | bytes 3981312 | tf_op jit(solution)/shard_map/all_gather | solution.py:100
  7.9 215.3 %all-gather.6.cloned.1.call-start = ((), (), s32[]{:S(2)}) async-start(), calls=%async_computation.10 | async-start | bytes 1327104 | tf_op jit(solution)/shard_map/all_gather | solution.py:101
  13.9 2.7 copy-start.42
  33.4 168.5 %copy-start.40 = (f32[768]{0:T(1024)}, f32[768]{0:T(1024)S(1)}, u32[]{:S(2)}) copy-start(f32[768]{0:T(1024)S(1)} %convert_element_type.167) | copy-start | bytes 9220
  35.3 166.6 %copy-start.46 = (f32[512]{0:T(512)}, f32[512]{0:T(512)S(1)}, u32[]{:S(2)}) copy-start(f32[512]{0:T(512)S(1)} %fusion.74) | copy-start | bytes 6148
  188.9 12.7 %copy-start.45 = (s32[512]{0:T(512)S(1)}, s32[512]{0:T(512)}, u32[]{:S(2)}) copy-start(s32[512]{0:T(512)} %param.17) | copy-start | bytes 6148
  188.9 13.1 %copy-start.14 = (bf16[512,768]{1,0:T(8,128)(2,1)S(1)}, bf16[512,768]{1,0:T(8,128)(2,1)}, u32[]{:S(2)}) copy-start(bf16[512,768]{1,0:T(8,128)(2,1)} %param.15) | copy-start | bytes 2359300
  201.8 24.0 %copy-start.29 = (f32[768]{0:T(1024)}, f32[768]{0:T(1024)S(1)}, u32[]{:S(2)}) copy-start(f32[768]{0:T(1024)S(1)} %convert_element_type.173) | copy-start | bytes 9220
  201.9 30.3 %copy-start.36 = (pred[8,192]{1,0:T(8,128)(4,1)}, pred[8,192]{1,0:T(8,128)(4,1)S(1)}, u32[]{:S(2)}) copy-start(pred[8,192]{1,0:T(8,128)(4,1)S(1)} %ge.44) | copy-start | bytes 4612
  207.4 8.6 copy-start.10
  207.7 8.3 copy-start.8
  209.4 8.5 copy-start.12
  216.0 4.5 copy-start.4
  216.0 4.7 copy-start.25
  217.9 5.3 copy-start.27
  223.2 2.5 copy-start.21
  225.7 6.4 copy-start.48
  225.8 6.4 copy-start.34
  227.2 5.0 copy-start.2
  232.2 32.8 %slice-start.5 = ((s8[4718592]{0:T(1024)(128)(4,1)}), s8[4194304]{0:T(1024)(128)(4,1)S(1)}, s32[]{:S(2)}) async-start(s8[4718592]{0:T(1024)(128)(4,1)} %bitcast.166), calls=%async_computation.22 | async-start | bytes 8388608
  232.2 32.8 %slice-start.6 = ((s8[4718592]{0:T(1024)(128)(4,1)}), s8[524288]{0:T(1024)(128)(4,1)S(1)}, s32[]{:S(2)}) async-start(s8[4718592]{0:T(1024)(128)(4,1)} %bitcast.166), calls=%async_computation.23 | async-start | bytes 1048576
  265.0 49.3 %copy-start.19 = (bf16[8,192,768]{2,1,0:T(8,128)(2,1)}, bf16[8,192,768]{2,1,0:T(8,128)(2,1)S(1)}, u32[]{:S(2)}) copy-start(bf16[8,192,768]{2,1,0:T(8,128)(2,1)S(1)} %all_to_all.16) | copy-start | bytes 7077892
  265.0 49.4 %copy-start.53 = (bf16[1,3072,768]{2,1,0:T(8,128)(2,1)S(1)}, bf16[1,3072,768]{2,1,0:T(8,128)(2,1)}, u32[]{:S(2)}) copy-start(bf16[1,3072,768]{2,1,0:T(8,128)(2,1)} %param.27) | copy-start | bytes 14155780
  314.4 7.7 copy-start.54
  380.5 8.3 copy-start.51
  383.8 45.7 %all-to-all-start.1 = ((bf16[8,2,73728]{2,1,0:T(2,128)(2,1)}), bf16[8,2,73728]{2,1,0:T(2,128)(2,1)S(1)}, u32[]{:S(2)}, u32[]{:S(2)}) async-start(bf16[8,2,73728]{2,1,0:T(2,128)(2,1)} %reshape.650), calls=%async_computation.1 | async-start | bytes 4718592 | tf_op jit(solution)/shard_map/all_to_all | solution.py:172
  420.0 8.9 copy-start.50
  420.0 9.0 copy-start.33
  420.0 9.0 copy-start.43
  420.1 9.0 copy-start.3
  420.1 9.3 copy-start.31
  436.9 5.2 copy-start.32
  436.9 5.2 copy-start.44
  448.2 5.6 copy-start.37
  453.8 34.5 %slice-start.3 = ((s8[4718592]{0:T(1024)(128)(4,1)}), s8[4194304]{0:T(1024)(128)(4,1)S(1)}, s32[]{:S(2)}) async-start(s8[4718592]{0:T(1024)(128)(4,1)} %bitcast.164), calls=%async_computation.20 | async-start | bytes 8388608
  453.8 34.5 %slice-start.4 = ((s8[4718592]{0:T(1024)(128)(4,1)}), s8[524288]{0:T(1024)(128)(4,1)S(1)}, s32[]{:S(2)}) async-start(s8[4718592]{0:T(1024)(128)(4,1)} %bitcast.164), calls=%async_computation.21 | async-start | bytes 1048576
  488.2 22.5 %copy-start.20 = (bf16[8,192,768]{2,1,0:T(8,128)(2,1)}, bf16[8,192,768]{2,1,0:T(8,128)(2,1)S(1)}, u32[]{:S(2)}) copy-start(bf16[8,192,768]{2,1,0:T(8,128)(2,1)S(1)} %all_to_all.17) | copy-start | bytes 7077892
  580.4 9.2 copy-start.26
  580.4 9.2 copy-start.28
  583.6 34.0 %all-to-all-start.3 = ((bf16[8,2,73728]{2,1,0:T(2,128)(2,1)}), bf16[8,2,73728]{2,1,0:T(2,128)(2,1)S(1)}, u32[]{:S(2)}, u32[]{:S(2)}) async-start(bf16[8,2,73728]{2,1,0:T(2,128)(2,1)} %reshape.648), calls=%async_computation.3 | async-start | bytes 4718592 | tf_op jit(solution)/shard_map/all_to_all | solution.py:177
  588.6 152.0 %reduce-scatter.16.cloned.1.call-start = ((), (), s32[]{:S(2)}) async-start(), calls=%async_computation.15 | async-start | bytes 442368
  590.8 163.2 %reduce-scatter.10.cloned.1.call-start = ((), (), s32[]{:S(2)}) async-start(), calls=%async_computation.12 | async-start | bytes 2654208 | tf_op jit(solution)/shard_map/reduce_scatter | solution.py:277
  644.1 18.1 %copy-start.7 = (f32[512,768]{1,0:T(8,128)S(1)}, f32[512,768]{1,0:T(8,128)}, u32[]{:S(2)}) copy-start(f32[512,768]{1,0:T(8,128)} %copy-done.6) | copy-start | bytes 4718596
  644.1 18.1 %copy-start.30 = (f32[768]{0:T(1024)S(1)}, f32[768]{0:T(1024)}, u32[]{:S(2)}) copy-start(f32[768]{0:T(1024)} %copy-done.29) | copy-start | bytes 9220
  644.1 18.2 %copy-start.35 = (f32[512]{0:T(512)S(1)}, f32[512]{0:T(512)}, u32[]{:S(2)}) copy-start(f32[512]{0:T(512)} %copy-done.34) | copy-start | bytes 6148
  666.9 4.6 copy-start.13
  671.4 112.1 %reduce-scatter.8.cloned.1.call-start = ((), (), s32[]{:S(2)}) async-start(), calls=%async_computation.11 | async-start | bytes 7962624 | tf_op jit(solution)/shard_map/reduce_scatter | solution.py:276
  671.5 10.8 %slice-start = ((s8[12582912]{0:T(1024)(128)(4,1)}), s8[4194304]{0:T(1024)(128)(4,1)S(1)}, s32[]{:S(2)}) async-start(s8[12582912]{0:T(1024)(128)(4,1)} %bitcast.129), calls=%async_computation.17 | async-start | bytes 8388608
  671.5 11.4 %slice-start.1 = ((s8[12582912]{0:T(1024)(128)(4,1)}), s8[4194304]{0:T(1024)(128)(4,1)S(1)}, s32[]{:S(2)}) async-start(s8[12582912]{0:T(1024)(128)(4,1)} %bitcast.129), calls=%async_computation.18 | async-start | bytes 8388608
  671.5 13.0 %slice-start.2 = ((s8[12582912]{0:T(1024)(128)(4,1)}), s8[4194304]{0:T(1024)(128)(4,1)S(1)}, s32[]{:S(2)}) async-start(s8[12582912]{0:T(1024)(128)(4,1)} %bitcast.129), calls=%async_computation.19 | async-start | bytes 8388608
  684.5 7.0 copy-start.9
  691.6 2.8 copy-start.5
  691.6 2.8 copy-start.11
  694.4 4.1 copy-start.17
  696.4 3.0 copy-start.15
  696.4 3.0 copy-start.41
  696.4 2.9 copy-start.47
  704.5 167.9 %reduce-scatter.14.cloned.1.call-start = ((), (), s32[]{:S(2)}) async-start(), calls=%async_computation.14 | async-start | bytes 5898240 | tf_op jit(solution)/shard_map/reduce_scatter | solution.py:270
  717.4 243.0 %reduce-scatter.12.cloned.1.call-start = ((), (), s32[]{:S(2)}) async-start(), calls=%async_computation.13 | async-start | bytes 5898240 | tf_op jit(solution)/shard_map/reduce_scatter | solution.py:267
  729.8 273.7 %all-reduce.12.cloned.1.call-start = ((), (), s32[]{:S(2)}) async-start(), calls=%async_computation.16 | async-start | bytes 1179648 | tf_op jit(solution)/shard_map/psum | solution.py:283
  741.5 44.1 %copy-start.18 = (bf16[12,64,512]{2,1,0:T(8,128)(2,1)S(1)}, bf16[12,64,512]{2,1,0:T(8,128)(2,1)}, u32[]{:S(2)}) copy-start(bf16[12,64,512]{2,1,0:T(8,128)(2,1)} %copy-done.17) | copy-start | bytes 2359300
  785.6 77.4 %copy-start.39 = (f32[512]{0:T(512)S(1)}, f32[512]{0:T(512)}, u32[]{:S(2)}) copy-start(f32[512]{0:T(512)} %copy-done.38) | copy-start | bytes 6148
  863.0 144.2 %copy-start.1 = (f32[32,12]{0,1:T(8,128)S(1)}, f32[32,12]{0,1:T(8,128)}, u32[]{:S(2)}) copy-start(f32[32,12]{0,1:T(8,128)} %param.23) | copy-start | bytes 4612
  (8 other events, 9.1 us)
Sparse Core Ops, SparseCore 0:
  9.9 35.0 all-gather.3
  46.9 24.1 all-gather.5
  592.5 35.7 reduce-scatter.15
  671.5 42.7 reduce-scatter.9
  718.1 65.4 reduce-scatter.7
  785.7 86.6 reduce-scatter.13
  874.7 85.6 reduce-scatter.11
  963.4 40.0 all-reduce.11
where the time goes:
time: 1030 us; the launch traced here: 1010 us
  local copies, waits for them, and re-layouts  325 us (32%)
  waiting for transfers between devices  188 us (18%)
  matrix products  180 us (17%)
  blocking collectives  178 us (17%)
  other arithmetic  116 us (11%)
  between operations  16.6 us (2%)
  starting transfers between devices  10.3 us (1%)
    unnamed x146, local copies, waits for them, and re-layouts  102 us
    reduce_scatter x1, waiting for transfers between devices, body(): lax.psum_scatter(grad_expert_in.astype(jnp.bfloat16), 'rep', scatter_dime...  85.1 us
    reshape x2, local copies, waits for them, and re-layouts, toeplitz_rows(): return flattened.reshape(lead + (length, 2 * length - 1))[..., length - 1:]  58.4 us
    dot_general x1, matrix products, expert_forward(): jnp.einsum('erd,edf->erf', expert_rows, expert_in, preferred_element_type...  49.3 us
    unnamed x6, other arithmetic  48.5 us
    psum x1, blocking collectives, body(): grad_rel_bias = lax.psum(grad_rel_bias, ('rep', 'shard'))  44.1 us
    psum x1, waiting for transfers between devices, body(): lax.psum(owned_qkv.astype(jnp.bfloat16), 'rep').astype(jnp.float32)  40.2 us
    convert_element_type x1, local copies, waits for them, and re-layouts, expert_forward(): expert_result = jnp.einsum('erf,efd->erd', act_low, expert_out, preferred...  33.8 us
  transfers between devices with their start and end apart: 10, of which 5 were waited for; matrix products, arithmetic and copies ran while one was open for 35% of the time, Pallas kernels for 0%

commit v1 on v0

v1 whole, which is shorter than its diff:
```python
import functools
import math

import jax
import jax.numpy as jnp
from jax import lax
from jax.experimental import pallas as pl
from jax.experimental.pallas import tpu as pltpu
from jax.sharding import PartitionSpec as P

F32 = jnp.float32
BF16 = jnp.bfloat16
EPS = 1e-06
NEG = -1e30
LANES = 128
HEAD_DIM = 64
GROUP = 256
VMEM_LIMIT = 60 * 1024 * 1024


def dot(a, b):
    return jnp.dot(a, b, preferred_element_type=F32)


def dot_nt(a, b):
    return lax.dot_general(a, b, (((1,), (1,)), ((), ())), preferred_element_type=F32)


def dot_tn(a, b):
    return lax.dot_general(a, b, (((0,), (0,)), ((), ())), preferred_element_type=F32)


def call(kernel, out_shape, **kw):
    flops = kw.pop("flops", 0)
    moved = kw.pop("moved", 0)
    return pl.pallas_call(
        kernel,
        out_shape=out_shape,
        compiler_params=pltpu.CompilerParams(vmem_limit_bytes=VMEM_LIMIT),
        cost_estimate=pl.CostEstimate(flops=flops, bytes_accessed=moved, transcendentals=0),
        **kw,
    )


def whole(shape):
    rank = len(shape)
    return pl.BlockSpec(shape, lambda *_: (0,) * rank)


def smem():
    return pl.BlockSpec(memory_space=pltpu.SMEM)


def sds(shape, dtype):
    return jax.ShapeDtypeStruct(shape, dtype)


def iota(shape, dim):
    return lax.broadcasted_iota(jnp.int32, shape, dim)


def prep_kernel(
    experts, capacity, routes_ref, seg_row, seg_col, rev_ref, bias_ref, cot_ref,
    table_ref, slot_row_ref, slot_col_ref, cot_out_ref, mask_scr, series_scr, extra_scr,
):
    step = pl.program_id(0)
    seq = cot_ref.shape[0]
    width = cot_ref.shape[1]
    per = cot_out_ref.shape[0]

    @pl.when(step == 0)
    def _():
        keep = (iota((seq, seq), 0) >= iota((seq, seq), 1)) & (seg_col[...] == seg_row[...])
        mask_scr[...] = jnp.where(keep, 0.0, NEG)
        rev = rev_ref[...]
        bias = bias_ref[...]
        series = jnp.zeros((bias.shape[0], seq), F32)
        for bucket in range(bias.shape[1]):
            series = jnp.where(rev == bucket, bias[:, bucket : bucket + 1], series)
        series_scr[...] = series
        first, second = routes_ref[0:1, :], routes_ref[1:2, :]
        ids = iota((experts, seq), 0)
        m0 = (ids == first).astype(F32)
        m1 = (ids == second).astype(F32)
        before = (iota((seq, seq), 0) < iota((seq, seq), 1)).astype(BF16)
        count = dot((m0 + m1).astype(BF16), before)
        rank0 = jnp.sum(count * m0, axis=0, keepdims=True)
        rank1 = jnp.sum(count * m1, axis=0, keepdims=True)
        r0, r1 = first.astype(F32), second.astype(F32)
        slot0 = jnp.where(rank0 < capacity, r0 * capacity + rank0, -1.0)
        slot1 = jnp.where(rank1 < capacity, r1 * capacity + rank1, -1.0)
        place = iota((LANES, seq), 0)
        rows = jnp.where(place == 0, slot0, -1.0)
        rows = jnp.where(place == 1, slot1, rows)
        rows = jnp.where(place == 2, r0, rows)
        rows = jnp.where(place == 3, r1, rows)
        slot_row_ref[...] = rows[0:8, :].astype(jnp.int32)
        cols = rows.T
        slot_col_ref[...] = cols
        lane = iota((seq, LANES), 1)
        extra_scr[0] = jnp.where(lane == 0, cols[:, 3:4], 0.0).astype(BF16)
        extra_scr[1] = jnp.where(lane == 0, cols[:, 2:3], 0.0).astype(BF16)

    row = series_scr[pl.ds(step, 1), :]
    table_ref[0] = pltpu.roll(jnp.broadcast_to(row, (seq, seq)), 0, 1, stride=1, stride_axis=0) + mask_scr[...]

    @pl.when(step < 8)
    def _():
        slots = iota((per, seq), 0) + step * per
        hit0 = (slots == slot_row_ref[0:1, :]).astype(F32)
        hit1 = (slots == slot_row_ref[1:2, :]).astype(F32)
        cot_out_ref[:, :width] = dot((hit0 + hit1).astype(BF16), cot_ref[...]).astype(BF16)
        cot_out_ref[:, width:] = (
            dot(hit0.astype(BF16), extra_scr[0]) + dot(hit1.astype(BF16), extra_scr[1])
        ).astype(BF16)


def prep(routes_t, segments, rev_buckets, rel_bias, cotangent, experts, capacity):
    seq, width = cotangent.shape
    heads = rel_bias.shape[1]
    buckets = rel_bias.shape[0]
    slots = experts * capacity
    per = slots // 8
    hp = -(-heads // 8) * 8
    bias_t = jnp.zeros((hp, buckets), F32).at[:heads].set(rel_bias.T)
    return call(
        functools.partial(prep_kernel, experts, capacity),
        [
            sds((heads, seq, seq), F32),
            sds((8, seq), jnp.int32),
            sds((seq, LANES), F32),
            sds((slots, width + LANES), BF16),
        ],
        grid=(heads,),
        in_specs=[
            whole((2, seq)), whole((1, seq)), whole((seq, 1)), whole((1, seq)),
            whole((hp, buckets)), whole((seq, width)),
        ],
        out_specs=[
            pl.BlockSpec((1, seq, seq), lambda h: (h, 0, 0)),
            whole((8, seq)),
            whole((seq, LANES)),
            pl.BlockSpec((per, width + LANES), lambda h: (jnp.minimum(h, 7), 0)),
        ],
        scratch_shapes=[
            pltpu.VMEM((seq, seq), F32),
            pltpu.VMEM((hp, seq), F32),
            pltpu.VMEM((2, seq, LANES), BF16),
        ],
        flops=2 * slots * seq * width,
        moved=heads * seq * seq * 4 + 4 * seq * width,
        name="prep",
    )(routes_t, segments[None, :], segments[:, None], rev_buckets[None, :], bias_t, cotangent)


def front_kernel(
    blocks, experts, me_ref, tokens_ref, table_ref, slot_row_ref, *refs,
):
    w_in = refs[:blocks]
    p_in = refs[blocks : 2 * blocks]
    (q_ref, k_ref, v_ref, lse_ref, att_ref, res_ref, n1_ref, n2_ref, logit_ref, sent_ref,
     qkv_ref, proj_ref, small_ref, small_t_ref) = refs[2 * blocks :]
    step = pl.program_id(0)
    last = pl.num_programs(0) - 1
    seq, width = tokens_ref.shape
    rows = w_in[0].shape[0]
    scale = HEAD_DIM ** (-0.5)

    @pl.when(step == 0)
    def _():
        me = me_ref[0]
        for j in range(blocks):
            start = pl.multiple_of((me ^ j) * rows, rows) if blocks > 1 else 0
            qkv_ref[pl.ds(start, rows), :] = w_in[j][:, : 3 * width]
            small_ref[pl.ds(start, rows), :] = w_in[j][:, 3 * width :]
            proj_ref[pl.ds(start, rows), :] = p_in[j][...]
        small_t_ref[...] = small_ref[...].astype(F32).T
        x = tokens_ref[...].astype(F32)
        r = lax.rsqrt(jnp.mean(x * x, axis=-1, keepdims=True) + EPS)
        n1_ref[...] = (x * r * small_t_ref[experts : experts + 1, :]).astype(BF16)
        lse_ref[...] = jnp.zeros_like(lse_ref)

    base = pl.multiple_of(step * GROUP, GROUP)
    n1 = n1_ref[...]
    q_ref[...] = dot(n1, qkv_ref[:, pl.ds(base, GROUP)]).astype(BF16)
    k_ref[...] = dot(n1, qkv_ref[:, pl.ds(width + base, GROUP)]).astype(BF16)
    v_ref[...] = dot(n1, qkv_ref[:, pl.ds(2 * width + base, GROUP)]).astype(BF16)

    half = seq // 2
    lane = iota((half, LANES), 1)
    for pair in range(GROUP // LANES):
        cols = slice(pair * LANES, (pair + 1) * LANES)
        for rb in range(2):
            span = (rb + 1) * half
            qrows = slice(rb * half, (rb + 1) * half)
            qp = q_ref[qrows, cols]
            kp = k_ref[:span, cols]
            vp = v_ref[:span, cols]
            mixed = []
            for parity in range(2):
                mine = (lane // HEAD_DIM) == parity
                qm = jnp.where(mine, qp, jnp.zeros_like(qp))
                s = dot_nt(qm, kp) * scale + table_ref[2 * pair + parity, qrows, :span]
                top = jnp.max(s, axis=-1, keepdims=True)
                e = jnp.exp(s - top)
                total = jnp.sum(e, axis=-1, keepdims=True)
                p = (e * (1.0 / total)).astype(BF16)
                mixed.append(dot(p, vp))
                head = step * (GROUP // HEAD_DIM) + 2 * pair + parity
                lse_ref[qrows, :] = jnp.where(lane == head, top + jnp.log(total), lse_ref[qrows, :])
            at = pl.multiple_of(base + pair * LANES, LANES)
            att_ref[qrows, pl.ds(at, LANES)] = jnp.where(lane < HEAD_DIM, mixed[0], mixed[1]).astype(BF16)

    @pl.when(step == last)
    def _():
        x = tokens_ref[...].astype(F32) + dot(att_ref[...], proj_ref[...])
        res_ref[...] = x
        r = lax.rsqrt(jnp.mean(x * x, axis=-1, keepdims=True) + EPS)
        n2 = (x * r * small_t_ref[experts + 1 : experts + 2, :]).astype(BF16)
        n2_ref[...] = n2
        logit_ref[...] = dot(n2, small_ref[...])
        per = sent_ref.shape[0] // 8
        for e in range(8):
            slots = iota((per, seq), 0) + e * per
            hit = (slots == slot_row_ref[0:1, :]) | (slots == slot_row_ref[1:2, :])
            sent_ref[e * per : (e + 1) * per, :] = dot(hit.astype(BF16), n2).astype(BF16)


def front(me, tokens, table, slot_row, w_blocks, p_blocks, experts, slots):
    seq, width = tokens.shape
    blocks = len(w_blocks)
    groups = width // GROUP
    per_group = GROUP // HEAD_DIM
    col = pl.BlockSpec((seq, GROUP), lambda g: (0, g))
    return call(
        functools.partial(front_kernel, blocks, experts),
        [
            sds((seq, width), BF16), sds((seq, width), BF16), sds((seq, width), BF16),
            sds((seq, LANES), F32), sds((seq, width), BF16), sds((seq, width), F32),
            sds((seq, width), BF16), sds((seq, width), BF16), sds((seq, LANES), F32),
            sds((slots, width), BF16),
            sds((width, 3 * width), BF16), sds((width, width), BF16), sds((width, LANES), BF16),
            sds((LANES, width), F32),
        ],
        grid=(groups,),
        in_specs=[
            smem(), whole((seq, width)),
            pl.BlockSpec((per_group, seq, seq), lambda g: (g, 0, 0)),
            whole((8, seq)),
        ]
        + [whole(b.shape) for b in w_blocks]
        + [whole(b.shape) for b in p_blocks],
        out_specs=[
            col, col, col,
            whole((seq, LANES)), whole((seq, width)), whole((seq, width)),
            whole((seq, width)), whole((seq, width)), whole((seq, LANES)),
            whole((slots, width)),
            whole((width, 3 * width)), whole((width, width)), whole((width, LANES)),
            whole((LANES, width)),
        ],
        flops=2 * seq * width * width * 4 + 2 * slots * seq * width + 8 * seq * seq * width,
        moved=30_000_000,
        name="front",
    )(me, tokens, table, slot_row, *w_blocks, *p_blocks)


def gelu_parts(v):
    size = jnp.abs(v) * (2.0 ** -0.5)
    t = 1.0 / (1.0 + 0.3275911 * size)
    bell = jnp.exp(-0.5 * v * v)
    poly = t * (
        0.5 * 0.254829592
        + t * (0.5 * -0.284496736 + t * (0.5 * 1.421413741 + t * (0.5 * -1.453152027 + t * (0.5 * 1.061405429))))
    )
    tail = poly * bell
    below = jnp.where(v < 0, tail, 1.0 - tail)
    return v * below, below + v * bell * (1.0 / math.sqrt(2.0 * math.pi))


def expert_kernel(first, ranks, tile, *refs):
    if first:
        (me_ref, rows_ref, cotx_ref, small_ref, win_ref, wout_ref,
         act_ref, gp_ref, buf_ref, rows_t, sg_ref, sg_t) = refs
    else:
        (rows_ref, sg_ref, rows_t, sg_t, win_ref, wout_ref, _a, _g,
         act_ref, gp_ref, buf_ref) = refs
    step = pl.program_id(0)
    total, width = rows_ref.shape
    if first:

        @pl.when(step == 0)
        def _():
            me = me_ref[0]
            for at in range(0, total, tile):
                here = slice(at, at + tile)
                logits = dot(rows_ref[here, :], small_ref[...])
                lane = iota((tile, LANES), 1)
                other_id = cotx_ref[here, width : width + 1].astype(F32).astype(jnp.int32)
                own = jnp.sum(jnp.where(lane == me, logits, 0.0), axis=1, keepdims=True)
                other = jnp.sum(jnp.where(lane == other_id, logits, 0.0), axis=1, keepdims=True)
                top = jnp.maximum(own, other)
                a, b = jnp.exp(own - top), jnp.exp(other - top)
                gate = a / (a + b)
                sg_ref[here, :] = (gate * cotx_ref[here, :width].astype(F32)).astype(BF16)
            rows_t[...] = rows_ref[...].T
            sg_t[...] = sg_ref[...].T

    w1 = win_ref[...]
    w2 = wout_ref[...]
    for at in range(0, total, tile):
        here = slice(at, at + tile)
        pre = dot(rows_ref[here, :], w1)
        ga = dot_nt(sg_ref[here, :], w2)
        act, slope = gelu_parts(pre)
        act_ref[here, :] = act.astype(BF16)
        gp_ref[here, :] = (ga * slope).astype(BF16)
    block = w1.shape[1]
    part = width // ranks
    gwin = dot(rows_t[...], gp_ref[...]).astype(BF16)
    gwout = dot(sg_t[...], act_ref[...]).T.astype(BF16)
    rank = lax.rem(step, ranks)
    cb = lax.div(step, ranks)
    lane0 = pl.multiple_of(rank * block, block)
    for dest in range(ranks):
        buf_ref[dest, cb, 0:part, pl.ds(lane0, block)] = gwin[dest * part : (dest + 1) * part, :]
    piece = block // ranks
    for i in range(ranks):
        for j in range(width // block):
            buf_ref[rank, cb, part + j * piece : part + (j + 1) * piece, i * block : (i + 1) * block] = gwout[
                i * piece : (i + 1) * piece, j * block : (j + 1) * block
            ]


def expert_chunk(first, ins, chunk, ranks, total, width, hidden):
    start, count = chunk
    block = 256
    per_rank = hidden // ranks // block
    part = width // ranks
    piece = block // ranks
    high = part + (width // block) * piece

    def at(s):
        return lax.rem(s, ranks) * per_rank + start + lax.div(s, ranks)

    win_spec = pl.BlockSpec((width, block), lambda s: (0, at(s)))
    wout_spec = pl.BlockSpec((block, width), lambda s: (at(s), 0))
    col = pl.BlockSpec((total, block), lambda s: (0, at(s)))
    outs = [
        sds((total, hidden), BF16),
        sds((total, hidden), BF16),
        sds((ranks, count, high, ranks * block), BF16),
    ]
    out_specs = [col, col, whole((ranks, count, high, ranks * block))]
    kw = {}
    if first:
        in_specs = [smem(), whole((total, width)), whole((total, width + LANES)), whole((width, LANES)), win_spec, wout_spec]
        outs += [sds((width, total), BF16), sds((total, width), BF16), sds((width, total), BF16)]
        out_specs += [whole((width, total)), whole((total, width)), whole((width, total))]
    else:
        in_specs = [
            whole((total, width)), whole((total, width)), whole((width, total)), whole((width, total)),
            win_spec, wout_spec,
            pl.BlockSpec(memory_space=pl.ANY), pl.BlockSpec(memory_space=pl.ANY),
        ]
        kw["input_output_aliases"] = {6: 0, 7: 1}
    return call(
        functools.partial(expert_kernel, first, ranks, 256),
        outs,
        grid=(count * ranks,),
        in_specs=in_specs,
        out_specs=out_specs,
        flops=8 * total * width * block * ranks * count,
        moved=20_000_000,
        name="experts",
        **kw,
    )(*ins)


def rows_kernel(transposed, a_ref, w_ref, o_ref):
    prod = dot_nt if transposed else dot
    o_ref[...] = prod(a_ref[...], w_ref[...]).astype(BF16)


def rows_out(transposed, a, w, width):
    total, hidden = a.shape
    tile = total // 8
    return call(
        functools.partial(rows_kernel, transposed),
        sds((total, width), BF16),
        grid=(8,),
        in_specs=[pl.BlockSpec((tile, hidden), lambda i: (i, 0)), whole(w.shape)],
        out_specs=pl.BlockSpec((tile, width), lambda i: (i, 0)),
        flops=2 * total * hidden * width,
        moved=2 * (total * hidden + hidden * width + total * width),
        name="expert_rows_back" if transposed else "expert_rows_out",
    )(a, w)


def norm_back(x, grad, gain, count):
    r = lax.rsqrt(jnp.mean(x * x, axis=-1, keepdims=True) + EPS)
    u = grad * gain
    inner = jnp.mean(u * x, axis=-1, keepdims=True)
    xr = x * r
    return r * u - (r * r * r) * x * inner, jnp.sum(grad * xr, axis=0, keepdims=True)


def mid_kernel(
    experts, ret_ref, back_ref, slot_ref, res_ref, logit_ref, cot_ref, n2_ref, att_ref,
    proj_ref, small_ref, small_t_ref, out_ref, gres_ref, gatt_ref, gproj_ref, gsmall_ref,
):
    seq, width = res_ref.shape
    slots = ret_ref.shape[0]
    lane = iota((seq, LANES), 1)
    spot = iota((seq, slots), 1)
    s0 = slot_ref[:, 0:1].astype(jnp.int32)
    s1 = slot_ref[:, 1:2].astype(jnp.int32)
    h0 = (spot == s0).astype(BF16)
    h1 = (spot == s1).astype(BF16)
    hot0 = lane == slot_ref[:, 2:3].astype(jnp.int32)
    hot1 = lane == slot_ref[:, 3:4].astype(jnp.int32)
    logits = logit_ref[...]
    c0 = jnp.sum(jnp.where(hot0, logits, 0.0), axis=1, keepdims=True)
    c1 = jnp.sum(jnp.where(hot1, logits, 0.0), axis=1, keepdims=True)
    top = jnp.maximum(c0, c1)
    e0, e1 = jnp.exp(c0 - top), jnp.exp(c1 - top)
    g0, g1 = e0 / (e0 + e1), e1 / (e0 + e1)
    cot = cot_ref[...].astype(F32)
    ret = ret_ref[...]
    p0 = dot(h0, ret)
    p1 = dot(h1, ret)
    x = res_ref[...]
    out_ref[...] = (x + (g0 * p0 + g1 * p1)).astype(BF16)
    d0 = jnp.sum(cot * p0, axis=1, keepdims=True)
    d1 = jnp.sum(cot * p1, axis=1, keepdims=True)
    mean = g0 * d0 + g1 * d1
    glog = jnp.where(hot0, g0 * (d0 - mean), 0.0) + jnp.where(hot1, g1 * (d1 - mean), 0.0)
    glog = glog.astype(BF16)
    grad = dot(h0 + h1, back_ref[...]) + dot_nt(glog, jnp.where(iota((width, LANES), 1) < experts, small_ref[...], jnp.zeros_like(small_ref[...])))
    gx, ggain = norm_back(x, grad, small_t_ref[experts + 1 : experts + 2, :], width)
    gres = gx + cot
    gres_ref[...] = gres
    branch = gres.astype(BF16)
    gproj_ref[...] = dot_tn(att_ref[...], branch).astype(BF16)
    gatt_ref[...] = dot_nt(branch, proj_ref[...]).astype(BF16)
    gain_rows = jnp.where(iota((LANES, width), 0) == experts + 1, ggain, 0.0)
    gsmall_ref[...] = dot_tn(n2_ref[...], glog) + gain_rows.T


def mid(experts, returned, back, slot_col, res, logits, cot, n2, att, proj, small, small_t):
    seq, width = res.shape
    ins = (returned, back, slot_col, res, logits, cot, n2, att, proj, small, small_t)
    return call(
        functools.partial(mid_kernel, experts),
        [
            sds((seq, width), BF16), sds((seq, width), F32), sds((seq, width), BF16),
            sds((width, width), BF16), sds((width, LANES), F32),
        ],
        in_specs=[whole(a.shape) for a in ins],
        out_specs=[
            whole((seq, width)), whole((seq, width)), whole((seq, width)),
            whole((width, width)), whole((width, LANES)),
        ],
        grid=(1,),
        flops=6 * returned.shape[0] * seq * width + 4 * seq * width * width,
        moved=15_000_000,
        name="token_side",
    )(*ins)


def tail_kernel(
    experts, buckets, tokens_ref, table_ref, q_ref, k_ref, v_ref, gatt_ref, lse_ref, n1_ref, gres_ref,
    wq_ref, wk_ref, wv_ref, small_t_ref, rev_ref, gproj_ref, gsmall_ref,
    pack_ref, gtok_ref, gbias_ref, acc_scr, diag_scr, g_scr, n1t_scr,
):
    step = pl.program_id(0)
    last = pl.num_programs(0) - 1
    seq, width = tokens_ref.shape
    half = seq // 2
    scale = HEAD_DIM ** (-0.5)

    @pl.when(step == 0)
    def _():
        acc_scr[...] = jnp.zeros_like(acc_scr)
        diag_scr[...] = jnp.zeros_like(diag_scr)
        n1t_scr[...] = n1_ref[...].T

    lane = iota((half, LANES), 1)
    full_lane = iota((seq, LANES), 1)
    for pair in range(GROUP // LANES):
        cols = slice(pair * LANES, (pair + 1) * LANES)
        dk = [jnp.zeros((seq, LANES), F32)] * 2
        dv = [jnp.zeros((seq, LANES), F32)] * 2
        skew = [jnp.zeros((LANES, seq), F32)] * 2
        for rb in range(2):
            span = (rb + 1) * half
            qrows = slice(rb * half, (rb + 1) * half)
            qp = q_ref[qrows, cols]
            gp = gatt_ref[qrows, cols]
            kp = k_ref[:span, cols]
            vp = v_ref[:span, cols]
            dq = []
            for parity in range(2):
                mine = (lane // HEAD_DIM) == parity
                head = step * (GROUP // HEAD_DIM) + 2 * pair + parity
                level = jnp.sum(jnp.where(lane == head, lse_ref[qrows, :], 0.0), axis=1, keepdims=True)
                qm = jnp.where(mine, qp, jnp.zeros_like(qp))
                gm = jnp.where(mine, gp, jnp.zeros_like(gp))
                s = dot_nt(qm, kp) * scale + table_ref[2 * pair + parity, qrows, :span]
                p = jnp.exp(s - level)
                dp = dot_nt(gm, vp)
                d = jnp.sum(p * dp, axis=1, keepdims=True)
                ds = p * (dp - d)
                low = ds.astype(BF16)
                dq.append(dot(low, kp) * scale)
                add_k = dot_tn(low, qp) * scale
                add_v = dot_tn(p.astype(BF16), gp)
                if span < seq:
                    zero = jnp.zeros((seq - span, LANES), F32)
                    add_k = jnp.concatenate([add_k, zero], axis=0)
                    add_v = jnp.concatenate([add_v, zero], axis=0)
                dk[parity] = dk[parity] + add_k
                dv[parity] = dv[parity] + add_v
                wide = low.astype(F32)
                if span < seq:
                    wide = jnp.concatenate([wide, jnp.zeros((half, seq - span), F32)], axis=1)
                for b in range(half // LANES):
                    shift = rb * half + b * LANES
                    rows = wide[b * LANES : (b + 1) * LANES, :]
                    if shift:
                        rows = jnp.concatenate([rows[:, shift:], rows[:, :shift]], axis=1)
                    skew[parity] = skew[parity] + rows
            g_scr[0, qrows, cols] = jnp.where(lane < HEAD_DIM, dq[0], dq[1]).astype(BF16)
        g_scr[1, :, cols] = jnp.where(full_lane < HEAD_DIM, dk[0], dk[1]).astype(BF16)
        g_scr[2, :, cols] = jnp.where(full_lane < HEAD_DIM, dv[0], dv[1]).astype(BF16)
        for parity in range(2):
            acc = skew[parity][0:8, :]
            for i in range(1, LANES // 8):
                acc = acc + pltpu.roll(skew[parity][i * 8 : (i + 1) * 8, :], seq - i * 8, 1)
            head = step * (GROUP // HEAD_DIM) + 2 * pair + parity
            diag_scr[pl.ds(pl.multiple_of(head * 8, 8), 8), :] = acc

    base = pl.multiple_of(step * GROUP, GROUP)
    w_refs = (wq_ref, wk_ref, wv_ref)
    n1t = n1t_scr[...]
    for i in range(3):
        g = g_scr[i]
        at = pl.multiple_of(i * width + base, GROUP)
        pack_ref[:, pl.ds(at, GROUP)] = dot(n1t, g).astype(BF16)
        acc_scr[...] += dot_nt(g, w_refs[i][...])

    @pl.when(step == last)
    def _():
        x = tokens_ref[...].astype(F32)
        gx, ggain = norm_back(x, acc_scr[...], small_t_ref[experts : experts + 1, :], width)
        gtok_ref[...] = (gx + gres_ref[...]).astype(BF16)
        gain_rows = jnp.where(iota((LANES, width), 0) == experts, ggain, 0.0)
        pack_ref[:, 3 * width : 4 * width] = gproj_ref[...]
        pack_ref[:, 4 * width :] = (gsmall_ref[...] + gain_rows.T).astype(BF16)
        count = diag_scr.shape[0]
        place = lax.rem(iota((count, seq), 0), 8)
        diag = diag_scr[...]
        total = jnp.where(place == 0, diag, 0.0)
        for r in range(1, 8):
            total = total + jnp.where(place == r, pltpu.roll(diag, seq - r, 1), 0.0)
        hot = (iota((buckets, seq), 0) == rev_ref[...]).astype(F32)
        per_row = lax.dot_general(
            total, hot, (((1,), (1,)), ((), ())), precision=lax.Precision.HIGHEST, preferred_element_type=F32
        )
        gbias_ref[...] = jnp.sum(per_row.reshape(count // 8, 8, buckets), axis=1)


def tail(experts, buckets, tokens, table, q, k, v, gatt, lse, n1, gres, qkv, small_t, rev_buckets, gproj, gsmall):
    seq, width = tokens.shape
    heads = table.shape[0]
    groups = width // GROUP
    per_group = GROUP // HEAD_DIM
    col = pl.BlockSpec((seq, GROUP), lambda g: (0, g))

    def wcol(i):
        return pl.BlockSpec((width, GROUP), lambda g: (0, i * groups + g))

    return call(
        functools.partial(tail_kernel, experts, buckets),
        [sds((width, 4 * width + LANES), BF16), sds((seq, width), BF16), sds((heads, buckets), F32)],
        grid=(groups,),
        in_specs=[
            whole((seq, width)),
            pl.BlockSpec((per_group, seq, seq), lambda g: (g, 0, 0)),
            col, col, col, col,
            whole((seq, LANES)), whole((seq, width)), whole((seq, width)),
            wcol(0), wcol(1), wcol(2),
            whole((LANES, width)), whole((1, seq)), whole((width, width)), whole((width, LANES)),
        ],
        out_specs=[whole((width, 4 * width + LANES)), whole((seq, width)), whole((heads, buckets))],
        scratch_shapes=[
            pltpu.VMEM((seq, width), F32),
            pltpu.VMEM((heads * 8, seq), F32),
            pltpu.VMEM((3, seq, GROUP), BF16),
            pltpu.VMEM((width, seq), BF16),
        ],
        flops=12 * seq * width * width + 20 * seq * seq * width,
        moved=30_000_000,
        name="tail",
    )(tokens, table, q, k, v, gatt, lse, n1, gres, qkv, qkv, qkv, small_t, rev_buckets[None, :], gproj, gsmall)


def swap(value, mask, size):
    return lax.ppermute(value, "shard", [(i, i ^ mask) for i in range(size)])


def gather_blocks(value, size):
    if size != 8:
        return [lax.all_gather(value, "shard", axis=0, tiled=True)]
    far = {j: swap(value, j, size) for j in (6, 2, 4)}
    far[0] = value
    near = {j ^ 1: swap(far[j], 1, size) for j in (0, 6, 2, 4)}
    return [far[j] if j in far else near[j] for j in range(8)]


def line_total(value, ranks):
    own = value.astype(F32)
    right = left = value
    gained = own
    for t in range(1, ranks):
        a = lax.ppermute(right, "rep", [(t - 1, t)])
        b = lax.ppermute(left, "rep", [(ranks - t, ranks - 1 - t)])
        gained = gained + (a.astype(F32) + b.astype(F32))
        right = (own + a.astype(F32)).astype(BF16)
        left = (own + b.astype(F32)).astype(BF16)
    return gained


def reduce_small(pack, me, size, ranks):
    if size != 8:
        owned = lax.psum_scatter(pack, "shard", scatter_dimension=0, tiled=True)
        return line_total(owned, ranks)
    rows = pack.shape[0] // size
    blocks = pack.reshape(4, 2, rows, pack.shape[1])
    core = me % 2
    chip = me // 2
    keep = lax.dynamic_index_in_dim(blocks, core, 1, keepdims=False)
    send = lax.dynamic_index_in_dim(blocks, 1 - core, 1, keepdims=False)
    both = keep.astype(F32) + swap(send, 1, size).astype(F32)
    low = both.astype(BF16)
    got = [
        swap(lax.dynamic_index_in_dim(low, chip ^ (j // 2), 0, keepdims=False), j, size).astype(F32)
        for j in (6, 2, 4)
    ]
    owned = lax.dynamic_index_in_dim(both, chip, 0, keepdims=False) + got[0] + got[1] + got[2]
    return line_total(owned.astype(BF16), ranks)


def body(
    tokens, cotangent, segments, buckets, routes, attn_gain, qkv_weight, proj_weight,
    rel_bias, moe_gain, router, expert_in, expert_out,
):
    seq, width = tokens.shape
    size = lax.axis_size("shard")
    ranks = lax.axis_size("rep")
    top = routes.shape[1]
    experts = expert_in.shape[0] * size
    hidden = expert_in.shape[2]
    capacity = 3 * seq * top // (2 * experts)
    slots = experts * capacity
    bucket_count = rel_bias.shape[0]
    me = lax.axis_index("shard").astype(jnp.int32)
    me_arr = me.reshape(1)
    own_rows = router.shape[0]

    small = jnp.concatenate(
        [router, attn_gain[:, None], moe_gain[:, None], jnp.zeros((own_rows, LANES - experts - 2), BF16)], axis=1
    )
    w_blocks = gather_blocks(jnp.concatenate([qkv_weight, small], axis=1), size)
    p_blocks = gather_blocks(proj_weight, size)
    rev_buckets = jnp.roll(buckets[::-1], 1)
    table, slot_row, slot_col, cot_slots = prep(
        routes.T, segments, rev_buckets, rel_bias, cotangent, experts, capacity
    )
    (q, k, v, lse, att, res, n1, n2, logits, sent, qkv_full, proj_full, small_full, small_t) = front(
        me_arr, tokens, table, slot_row, w_blocks, p_blocks, experts, slots
    )

    def exchange(value):
        wide = value.shape[1]
        moved = lax.all_to_all(
            value.reshape(size, slots // size, wide), "shard", split_axis=0, concat_axis=0, tiled=True
        )
        return moved.reshape(slots, wide)

    cot_rows = exchange(cot_slots)
    rows = exchange(sent)
    win = expert_in[0]
    wout = expert_out[0]
    per_rank = hidden // ranks // 256
    act, gpre, buf0, rows_t, sg, sg_t = expert_chunk(
        True, (me_arr, rows, cot_rows, small_full, win, wout), (0, 1), ranks, slots, width, hidden
    )
    act, gpre, buf1 = expert_chunk(
        False, (rows, sg, rows_t, sg_t, win, wout, act, gpre), (1, per_rank - 1), ranks, slots, width, hidden
    )
    result = rows_out(False, act, wout, width)
    returned = exchange(result)
    grad_sent = rows_out(True, gpre, win, width)
    back = exchange(grad_sent)

    def scatter(buf):
        count, high, wide = buf.shape[1:]
        return lax.psum_scatter(
            buf.reshape(ranks * count * high, wide), "rep", scatter_dimension=0, tiled=True
        ).reshape(count, high, wide)

    done = [scatter(buf0), scatter(buf1)]
    output, gres, gatt, gproj, gsmall = mid(
        experts, returned, back, slot_col, res, logits, cotangent, n2, att, proj_full, small_full, small_t
    )
    pack, grad_tokens, gbias = tail(
        experts, bucket_count, tokens, table, q, k, v, gatt, lse, n1, gres, qkv_full, small_t,
        rev_buckets, gproj, gsmall,
    )
    grad_rel_bias = lax.psum(gbias, ("rep", "shard")).T
    owned = reduce_small(pack, me, size, ranks)

    pieces = jnp.concatenate(done, axis=0).astype(F32)
    part = width // ranks
    gin = pieces[:, :part, :].reshape(per_rank, part, ranks, 256)
    grad_in = gin.transpose(1, 2, 0, 3).reshape(1, part, hidden)
    piece = 256 // ranks
    gout = pieces[:, part:, :].reshape(per_rank, width // 256, piece, ranks, 256)
    grad_out = gout.transpose(0, 3, 2, 1, 4).reshape(1, hidden // ranks, width)
    return (
        output,
        grad_tokens,
        owned[:, : 3 * width],
        owned[:, 3 * width : 4 * width],
        owned[:, 4 * width : 4 * width + experts],
        owned[:, 4 * width + experts],
        owned[:, 4 * width + experts + 1],
        grad_rel_bias,
        grad_in,
        grad_out,
    )


def solution(mesh):
    both = P(("rep", "shard"), None)
    return jax.shard_map(
        body,
        mesh=mesh,
        in_specs=(
            both, both, P(("rep", "shard")), P(), both,
            P("shard"), P("shard", None), P("shard", None), P(), P("shard"), P("shard", None),
            P("shard", None, None), P("shard", None, None),
        ),
        out_specs=(
            both, both, P("shard", None), P("shard", None), P("shard", None), P("shard"), P("shard"), P(),
            P("shard", "rep", None), P("shard", "rep", None),
        ),
        check_vma=False,
    )
```

time: 1030 us -> 513 us (0.50)
  local copies, waits for them, and re-layouts: 325 us -> 33.1 us
  matrix products: 180 us -> 0 us
  Pallas kernels: 0 us -> 159 us
  other arithmetic: 116 us -> 14.8 us
  blocking collectives: 178 us -> 105 us
  waiting for transfers between devices: 188 us -> 141 us
  starting transfers between devices: 10.3 us -> 37 us
    dot_general x22 -> x0, matrix products: 179 us -> none  [the longest x1 49.3 us: expert_forward(): jnp.einsum('erd,edf->erf', expert_rows, expert_in, preferred_element_type...]
    pallas_call x0 -> x8, Pallas kernels: none -> 159 us  [the longest x2 55.7 us: expert_chunk(): call(functools.partial(expert_kernel, first, ranks, 256), outs, grid=(cou...]
    reduce_scatter x4 -> x2, waiting for transfers between devices: 120 us -> 0.01 us  [scatter(): lax.psum_scatter(buf.reshape(ranks * count * high, wide), 'rep', scatter_...]
    ppermute x0 -> x24, waiting for transfers between devices: none -> 102 us  [the longest x18 89.6 us: swap(): return lax.ppermute(value, 'shard', [(i, i ^ mask) for i in range(size)])]
    unnamed x146 -> x34, local copies, waits for them, and re-layouts: 102 us -> 2.42 us
    convert_element_type x6 -> x0, local copies, waits for them, and re-layouts: 78.7 us -> none  [the longest x1 33.8 us: expert_forward(): expert_result = jnp.einsum('erf,efd->erd', act_low, expert_out, preferred...]
    unnamed x6 -> x0, other arithmetic: 48.5 us -> none
    reshape x2 -> x4, local copies, waits for them, and re-layouts: 58.4 us -> 11.6 us  [the longest x1 3.7 us: body(): pieces[:, part:, :].reshape(per_rank, width // 256, piece, ranks, 256)]
  transfers between devices with their start and end apart: 10 -> 29, of which waited for: 5 -> 11; matrix products, arithmetic and copies ran while one was open for 35% -> 4% of each run, Pallas kernels for 0% -> 25%
where the time goes in v1:
time: 513 us; the launch traced here: 504 us
  Pallas kernels  159 us (31%)
  waiting for transfers between devices  141 us (27%)
  blocking collectives  105 us (20%)
  starting transfers between devices  37 us (7%)
  local copies, waits for them, and re-layouts  33.1 us (6%)
  other arithmetic  14.8 us (3%)
  between operations  14.6 us (3%)
    ppermute x18, waiting for transfers between devices, swap(): return lax.ppermute(value, 'shard', [(i, i ^ mask) for i in range(size)])  89.6 us
    psum x1, blocking collectives, body(): grad_rel_bias = lax.psum(gbias, ('rep', 'shard')).T  70.4 us
    pallas_call x2, Pallas kernels, expert_chunk(): call(functools.partial(expert_kernel, first, ranks, 256), outs, grid=(cou...  55.7 us
    all_to_all x3, waiting for transfers between devices, exchange(): lax.all_to_all(value.reshape(size, slots // size, wide), 'shard', split_a...  38.5 us
    all_to_all x1, blocking collectives, exchange(): lax.all_to_all(value.reshape(size, slots // size, wide), 'shard', split_a...  34.1 us
    pallas_call x2, Pallas kernels, rows_out(): call(functools.partial(rows_kernel, transposed), sds((total, width), BF16...  30.1 us
    pallas_call x1, Pallas kernels, tail(): call(functools.partial(tail_kernel, experts, buckets), [sds((width, 4 * w...  25.5 us
    pallas_call x1, Pallas kernels, front(): call(functools.partial(front_kernel, blocks, experts), [sds((seq, width),...  24 us
  transfers between devices with their start and end apart: 29, of which 11 were waited for; matrix products, arithmetic and copies ran while one was open for 4% of the time, Pallas kernels for 25%

profile of v1, /device:TPU:4, one launch (start us, length us, event | category | flops | bytes accessed | tf_op | source)
XLA Modules:
  0.0 504.3 jit_solution(16340622388957455016)
XLA Ops:
  7.2 0.8 slice.50
  7.9 1.2 slice.49
  9.3 1.5 copy.53.seg_col
  10.8 1.3 pad_add_fusion
  12.1 1.3 scatter.4.bias_ref
  13.4 11.6 %prep.1 = (f32[12,512,512]{2,1,0:T(8,128)}, s32[8,512]{1,0:T(8,128)}, f32[512,128]{1,0:T(8,128)}, bf16[1536,896]{1,0:T(8,128)(2,1)}) custom-call(s32[2,512]{1,0:T(2,128)} %bitcast.78, s32[1,512]{1,0:T(1,128)} %bitcast.69, s32[512,1]{1,0:T(8,128)} %copy.53.seg_col, s32[1,512]{1,0:T(1,128)} %bitcast.63, f32[16,32]{1,0:T(8,128)} %scatter.4.bias_ref, ...), custom_call_target="tpu_custom_call" | custom-call | flops 1207959552 | bytes 14155776 | tf_op jit(solution)/shard_map/prep/pallas_call | solution.py:126
  25.0 4.4 all-to-all-start.1
  29.8 1.1 concatenate.13.refs_0_
  30.9 1.5 collective-permute-start.1
  32.5 0.6 collective-permute-start.3
  33.0 1.5 collective-permute-start.5
  34.6 2.8 collective-permute-start.12
  37.4 49.4 %collective-permute-done.10.refs_12_ = bf16[96,768]{1,0:T(8,128)(2,1)S(1)} collective-permute-done((bf16[96,768]{1,0:T(8,128)(2,1)S(1)}, bf16[96,768]{1,0:T(8,128)(2,1)S(1)}, u32[]{:S(2)}, u32[]{:S(2)}) %collective-permute-start.10) | collective-permute-done | bytes 147488 | tf_op jit(solution)/shard_map/ppermute | solution.py:608
  86.8 1.5 collective-permute-start.8
  88.3 4.3 collective-permute-done.8.refs_10_
  92.6 0.5 collective-permute-start.2
  93.8 1.7 collective-permute-done.11.refs_13_
  95.6 1.3 collective-permute-done.13.refs_15_
  97.0 1.6 collective-permute-done.9.refs_11_
  98.6 24.0 %front.1 = (bf16[512,768]{1,0:T(8,128)(2,1)}, bf16[512,768]{1,0:T(8,128)(2,1)}, bf16[512,768]{1,0:T(8,128)(2,1)}, f32[512,128]{1,0:T(8,128)}, bf16[512,768]{1,0:...) custom-call(s32[1]{0:T(128)} %bitcast.me_ref.refs_0_, ...), custom_call_target="tpu_custom_call" | custom-call | flops 5234491392 | bytes 30000000 | tf_op jit(solution)/shard_map/front/pallas_call | solution.py:235
  122.7 34.1 %all_to_all.20 = bf16[8,192,768]{2,1,0:T(8,128)(2,1)} all-to-all(bf16[8,192,768]{2,1,0:T(8,128)(2,1)} %bitcast.57), channel_id=1, replica_groups=mesh['rep'=4,'shard'=8] {'shard'}, dimensions={0} | all-to-all | bytes 4718592 | tf_op jit(solution)/shard_map/all_to_all | solution.py:685
  156.7 22.1 %experts.2 = (bf16[1536,3072]{1,0:T(8,128)(2,1)}, bf16[1536,3072]{1,0:T(8,128)(2,1)}, bf16[4,1,384,1024]{3,2,1,0:T(8,128)(2,1)}, bf16[768,1536]{1,0:T(8,128)(2,1...) custom-call(s32[1]{0:T(128)} %bitcast.me_ref.refs_0_, bf16[1536,768]{1,0:T(8,128)(2,1)} %bitcast.58, ...), custom_call_target="tpu_custom_call" | custom-call | flops 9663676416 | bytes 20000000 | tf_op jit(solution)/shard_map/experts/pallas_call | solution.py:366
  178.9 33.6 %experts.3 = (bf16[1536,3072]{1,0:T(8,128)(2,1)}, bf16[1536,3072]{1,0:T(8,128)(2,1)}, bf16[4,2,384,1024]{3,2,1,0:T(8,128)(2,1)}) custom-call(bf16[1536,768]{1,0:T(8,128)(2,1)} %bitcast.59, bf16[1536,768]{1,0:T(8,128)(2,1)} %get-tuple-element.62.refs_1_, bf16[768,1536]{1,0:T(8,128)(2,1)} %get-tuple-element.63.refs_2_, ...), custom_call_target="tpu_custom_call", output_to_operand_aliasing={{0}: (6, {}), {1}: (7, {})} | custom-call | flops 19327352832 | bytes 20000000 | tf_op jit(solution)/shard_map/experts/pallas_call | solution.py:366
  212.5 13.2 %expert_rows_out.1 = bf16[1536,768]{1,0:T(8,128)(2,1)} custom-call(bf16[1536,3072]{1,0:T(8,128)(2,1)} %get-tuple-element.67.a_ref, bf16[3072,768]{1,0:T(8,128)(2,1)} %bitcast.74), custom_call_target="tpu_custom_call" | custom-call | flops 7247757312 | bytes 16515072 | tf_op jit(solution)/shard_map/expert_rows_out/pallas_call | solution.py:387
  225.7 5.0 all-to-all-start.2
  230.8 16.8 %expert_rows_back.1 = bf16[1536,768]{1,0:T(8,128)(2,1)} custom-call(bf16[1536,3072]{1,0:T(8,128)(2,1)} %get-tuple-element.68.a_ref, bf16[768,3072]{1,0:T(8,128)(2,1)} %bitcast.77), custom_call_target="tpu_custom_call" | custom-call | flops 7247757312 | bytes 16515072 | tf_op jit(solution)/shard_map/expert_rows_back/pallas_call | solution.py:387
  247.6 11.1 %all-to-all-done.2 = bf16[8,192,768]{2,1,0:T(8,128)(2,1)S(1)} async-done(((bf16[8,192,768]{2,1,0:T(8,128)(2,1)}), bf16[8,192,768]{2,1,0:T(8,128)(2,1)S(1)}, u32[]{:S(2)}, u32[]{:S(2)}) %all-to-all-start.2) | async-done | bytes 2359328 | tf_op jit(solution)/shard_map/all_to_all | solution.py:685
  258.7 1.4 copy-done.3
  260.2 5.8 %all-to-all-start.3 = ((bf16[8,192,768]{2,1,0:T(8,128)(2,1)}), bf16[8,192,768]{2,1,0:T(8,128)(2,1)}, u32[]{:S(2)}, u32[]{:S(2)}) async-start(bf16[8,192,768]{2,1,0:T(8,128)(2,1)} %bitcast.56), calls=%async_computation.3 | async-start | bytes 4718592 | tf_op jit(solution)/shard_map/all_to_all | solution.py:685
  266.6 27.4 %all-to-all-done.3 = bf16[8,192,768]{2,1,0:T(8,128)(2,1)} async-done(((bf16[8,192,768]{2,1,0:T(8,128)(2,1)}), bf16[8,192,768]{2,1,0:T(8,128)(2,1)}, u32[]{:S(2)}, u32[]{:S(2)}) %all-to-all-start.3) | async-done | bytes 2359328 | tf_op jit(solution)/shard_map/all_to_all | solution.py:685
  294.0 12.6 %token_side.1 = (bf16[512,768]{1,0:T(8,128)(2,1)}, f32[512,768]{1,0:T(8,128)}, bf16[512,768]{1,0:T(8,128)(2,1)}, bf16[768,768]{1,0:T(8,128)(2,1)}, f32[768,128]{1,0:T(8,128)}) custom-call(bf16[1536,768]{1,0:T(8,128)(2,1)} %bitcast.55, bf16[1536,768]{1,0:T(8,128)(2,1)} %bitcast.17.back_ref, f32[512,128]{1,0:T(8,128)} %get-tuple-element.69.slot_ref, ...), custom_call_target="tpu_custom_call" | custom-call | flops 4831838208 | bytes 15000000 | tf_op jit(solution)/shard_map/token_side/pallas_call | solution.py:452
  306.6 25.5 %tail.1 = (bf16[768,3200]{1,0:T(8,128)(2,1)}, bf16[512,768]{1,0:T(8,128)(2,1)}, f32[12,32]{1,0:T(8,128)}) custom-call(bf16[512,768]{1,0:T(8,128)(2,1)} %tokens_ref.3, f32[12,512,512]{2,1,0:T(8,128)} %get-tuple-element.57.table_ref, bf16[512,768]{1,0:T(8,128)(2,1)} %get-tuple-element.77.q_ref, bf16[512,768]{1,0:T(8,128)(2,1)} %get-tuple-element.78.k_ref, ...), custom_call_target="tpu_custom_call" | custom-call | flops 7650410496 | bytes 30000000 | tf_op jit(solution)/shard_map/tail/pallas_call | solution.py:582
  332.1 1.9 dynamic-slice_bitcast_fusion
  334.1 4.8 collective-permute-done.14
  338.8 5.2 %fusion.9 = (bf16[4,96,3200]{2,1,0:T(8,128)(2,1)S(1)}, f32[4,96,3200]{2,1,0:T(8,128)}) fusion(bf16[4,96,3200]{2,1,0:T(8,128)(2,1)} %collective-permute-done.14, bf16[4,2,96,3200]{3,2,1,0:T(8,128)(2,1)} %bitcast.51, s32[]{:T(128)S(6)} %select_n.33), kind=kLoop, calls=%fused_computation.26 | loop fusion | flops 4915200 | bytes 12288004 | tf_op jit(solution)/shard_map/convert_element_type | solution.py:644
  344.2 1.5 collective-permute-start.15
  345.7 1.5 collective-permute-start.16
  347.2 0.5 collective-permute-start.17
  347.8 14.2 %collective-permute-done.15 = bf16[96,3200]{1,0:T(8,128)(2,1)S(1)} collective-permute-done((bf16[96,3200]{1,0:T(8,128)(2,1)S(1)}, bf16[96,3200]{1,0:T(8,128)(2,1)S(1)}, u32[]{:S(2)}, u32[]{:S(2)}) %collective-permute-start.15) | collective-permute-done | bytes 614432 | tf_op jit(solution)/shard_map/ppermute | solution.py:608
  361.9 12.4 %collective-permute-done.16 = bf16[96,3200]{1,0:T(8,128)(2,1)S(1)} collective-permute-done((bf16[96,3200]{1,0:T(8,128)(2,1)S(1)}, bf16[96,3200]{1,0:T(8,128)(2,1)S(1)}, u32[]{:S(2)}, u32[]{:S(2)}) %collective-permute-start.16) | collective-permute-done | bytes 614432 | tf_op jit(solution)/shard_map/ppermute | solution.py:608
  374.3 1.8 fusion.8
  376.1 3.5 collective-permute-start.18
  379.6 0.7 collective-permute-start.19
  380.3 12.5 %collective-permute-done.18 = bf16[96,3200]{1,0:T(8,128)(2,1)S(1)} collective-permute-done((bf16[96,3200]{1,0:T(8,128)(2,1)S(1)}, bf16[96,3200]{1,0:T(8,128)(2,1)S(1)}, u32[]{:S(2)}, u32[]{:S(2)}) %collective-permute-start.18) | collective-permute-done | bytes 614432 | tf_op jit(solution)/shard_map/ppermute | solution.py:625
  393.0 0.7 collective-permute-start.20
  393.8 1.2 fusion.4
  395.0 0.7 collective-permute-start.21
  395.7 1.5 collective-permute-start.22
  397.2 1.0 fusion.5
  398.2 1.3 collective-permute-start.23
  399.5 70.4 %psum.7 = f32[32,12]{0,1:T(8,128)} all-reduce(f32[32,12]{0,1:T(8,128)S(1)} %bitcast.66), channel_id=1, replica_groups=mesh['rep'=4,'shard'=8] {'rep','shard'}, use_global_device_ids=true, to_apply=%region_0.1 | all-reduce | flops 384 | bytes 3072 | tf_op jit(solution)/shard_map/psum | solution.py:720
  470.0 2.2 fusion.1
  472.2 1.0 slice.59
  473.1 0.7 slice.60
  473.9 0.7 copy.59
  474.5 0.7 slice_reduce_fusion
  475.2 1.9 maximum_convert_fusion
  477.2 2.0 fusion.10
  479.1 2.1 reshape.116
  481.2 3.3 copy.57
  484.5 2.9 reshape.117
  487.4 3.7 reshape.118
  491.1 3.3 copy.58
  494.4 2.9 reshape.119
  (69 shorter events, 2.8 us)
Async XLA Ops:
  25.0 4.4 copy-start.6
  25.0 4.5 copy-start.7
  25.0 4.6 copy-start.8
  25.0 9.5 %copy-start.9 = (bf16[96,768]{1,0:T(8,128)(2,1)S(1)}, bf16[96,768]{1,0:T(8,128)(2,1)}, u32[]{:S(2)}) copy-start(bf16[96,768]{1,0:T(8,128)(2,1)} %refs_8_.1) | copy-start | bytes 442372
  25.0 97.6 %all-to-all-start.1 = ((bf16[8,192,896]{2,1,0:T(8,128)(2,1)}), bf16[8,192,896]{2,1,0:T(8,128)(2,1)S(1)}, u32[]{:S(2)}, u32[]{:S(2)}) async-start(bf16[8,192,896]{2,1,0:T(8,128)(2,1)} %bitcast.54), calls=%async_computation.1 | async-start | bytes 5505024 | tf_op jit(solution)/shard_map/all_to_all | solution.py:685
  29.4 445.8 %reduce-scatter.3.cloned.1.call-start = ((), (), s32[]{:S(2)}) async-start(), calls=%async_computation.6 | async-start | bytes 3932160 | tf_op jit(solution)/shard_map/reduce_scatter | solution.py:708
  30.9 67.7 %copy-start.4 = (bf16[96,2432]{1,0:T(8,128)(2,1)}, bf16[96,2432]{1,0:T(8,128)(2,1)S(1)}, u32[]{:S(2)}) copy-start(bf16[96,2432]{1,0:T(8,128)(2,1)S(1)} %concatenate.13.refs_0_) | copy-start | bytes 1400836
  30.9 61.7 %collective-permute-start.1 = (bf16[96,2432]{1,0:T(8,128)(2,1)S(1)}, bf16[96,2432]{1,0:T(8,128)(2,1)}, u32[]{:S(2)}, u32[]{:S(2)}) collective-permute-start(bf16[96,2432]{1,0:T(8,128)(2,1)S(1)} %concatenate.13.refs_0_), channel_id=1, source_target_pairs={{0,2},{1,3},{2,0},{3,1},{4,6},{5,7},{6,4},{7,5},{8,10},{9,11},{10,... | collective-permute-start | bytes 1400840 | tf_op jit(solution)/shard_map/ppermute | solution.py:608
  32.5 60.6 %collective-permute-start.3 = (bf16[96,2432]{1,0:T(8,128)(2,1)S(1)}, bf16[96,2432]{1,0:T(8,128)(2,1)}, u32[]{:S(2)}, u32[]{:S(2)}) collective-permute-start(bf16[96,2432]{1,0:T(8,128)(2,1)S(1)} %concatenate.13.refs_0_), channel_id=1, source_target_pairs={{0,4},{1,5},{2,6},{3,7},{4,0},{5,1},{6,2},{7,3},{8,12},{9,13},{10,... | collective-permute-start | bytes 1400840 | tf_op jit(solution)/shard_map/ppermute | solution.py:608
  33.0 60.2 %collective-permute-start.5 = (bf16[96,2432]{1,0:T(8,128)(2,1)S(1)}, bf16[96,2432]{1,0:T(8,128)(2,1)}, u32[]{:S(2)}, u32[]{:S(2)}) collective-permute-start(bf16[96,2432]{1,0:T(8,128)(2,1)S(1)} %concatenate.13.refs_0_), channel_id=1, source_target_pairs={{0,6},{1,7},{2,4},{3,5},{4,2},{5,3},{6,0},{7,1},{8,14},{9,15},{10,... | collective-permute-start | bytes 1400840 | tf_op jit(solution)/shard_map/ppermute | solution.py:608
  34.5 52.3 %collective-permute-start.10 = (bf16[96,768]{1,0:T(8,128)(2,1)S(1)}, bf16[96,768]{1,0:T(8,128)(2,1)S(1)}, u32[]{:S(2)}, u32[]{:S(2)}) collective-permute-start(bf16[96,768]{1,0:T(8,128)(2,1)S(1)} %copy-done.9), channel_id=1, source_target_pairs={{0,4},{1,5},{2,6},{3,7},{4,0},{5,1},{6,2},{7,3},{8,12},{9,13},{10,... | collective-permute-start | bytes 442376 | tf_op jit(solution)/shard_map/ppermute | solution.py:608
  34.6 53.7 %collective-permute-start.12 = (bf16[96,768]{1,0:T(8,128)(2,1)S(1)}, bf16[96,768]{1,0:T(8,128)(2,1)S(1)}, u32[]{:S(2)}, u32[]{:S(2)}) collective-permute-start(bf16[96,768]{1,0:T(8,128)(2,1)S(1)} %copy-done.9), channel_id=1, source_target_pairs={{0,6},{1,7},{2,4},{3,5},{4,2},{5,3},{6,0},{7,1},{8,14},{9,15},{10,... | collective-permute-start | bytes 442376 | tf_op jit(solution)/shard_map/ppermute | solution.py:608
  86.8 6.8 %copy-start.10 = (bf16[96,768]{1,0:T(8,128)(2,1)}, bf16[96,768]{1,0:T(8,128)(2,1)S(1)}, u32[]{:S(2)}) copy-start(bf16[96,768]{1,0:T(8,128)(2,1)S(1)} %collective-permute-done.10.refs_12_) | copy-start | bytes 442372
  86.8 5.8 %collective-permute-start.8 = (bf16[96,768]{1,0:T(8,128)(2,1)S(1)}, bf16[96,768]{1,0:T(8,128)(2,1)}, u32[]{:S(2)}, u32[]{:S(2)}) collective-permute-start(bf16[96,768]{1,0:T(8,128)(2,1)S(1)} %copy-done.9), channel_id=1, source_target_pairs={{0,2},{1,3},{2,0},{3,1},{4,6},{5,7},{6,4},{7,5},{8,10},{9,11},{10,... | collective-permute-start | bytes 442376 | tf_op jit(solution)/shard_map/ppermute | solution.py:608
  88.3 7.2 %copy-start.11 = (bf16[96,768]{1,0:T(8,128)(2,1)}, bf16[96,768]{1,0:T(8,128)(2,1)S(1)}, u32[]{:S(2)}) copy-start(bf16[96,768]{1,0:T(8,128)(2,1)S(1)} %collective-permute-done.12.refs_14_) | copy-start | bytes 442372
  88.3 5.4 %collective-permute-start.7 = (bf16[96,768]{1,0:T(8,128)(2,1)S(1)}, bf16[96,768]{1,0:T(8,128)(2,1)S(1)}, u32[]{:S(2)}, u32[]{:S(2)}) collective-permute-start(bf16[96,768]{1,0:T(8,128)(2,1)S(1)} %copy-done.9), channel_id=1, source_target_pairs={{0,1},{1,0},{2,3},{3,2},{4,5},{5,4},{6,7},{7,6},{8,9},{9,8},{10,11... | collective-permute-start | bytes 442376 | tf_op jit(solution)/shard_map/ppermute | solution.py:608
  92.6 6.0 %collective-permute-start = (bf16[96,2432]{1,0:T(8,128)(2,1)S(1)}, bf16[96,2432]{1,0:T(8,128)(2,1)}, u32[]{:S(2)}, u32[]{:S(2)}) collective-permute-start(bf16[96,2432]{1,0:T(8,128)(2,1)S(1)} %concatenate.13.refs_0_), channel_id=1, source_target_pairs={{0,1},{1,0},{2,3},{3,2},{4,5},{5,4},{6,7},{7,6},{8,9},{9,8},{10,11... | collective-permute-start | bytes 1400840 | tf_op jit(solution)/shard_map/ppermute | solution.py:608
  92.6 6.0 %collective-permute-start.2 = (bf16[96,2432]{1,0:T(8,128)(2,1)}, bf16[96,2432]{1,0:T(8,128)(2,1)}, u32[]{:S(2)}, u32[]{:S(2)}) collective-permute-start(bf16[96,2432]{1,0:T(8,128)(2,1)} %collective-permute-done.1.refs_2_), channel_id=1, source_target_pairs={{0,1},{1,0},{2,3},{3,2},{4,5},{5,4},{6,7},{7,6},{8,9},{9,8},{10,11... | collective-permute-start | bytes 1400840 | tf_op jit(solution)/shard_map/ppermute | solution.py:608
  93.1 5.5 %collective-permute-start.4 = (bf16[96,2432]{1,0:T(8,128)(2,1)}, bf16[96,2432]{1,0:T(8,128)(2,1)}, u32[]{:S(2)}, u32[]{:S(2)}) collective-permute-start(bf16[96,2432]{1,0:T(8,128)(2,1)} %collective-permute-done.3.refs_4_), channel_id=1, source_target_pairs={{0,1},{1,0},{2,3},{3,2},{4,5},{5,4},{6,7},{7,6},{8,9},{9,8},{10,11... | collective-permute-start | bytes 1400840 | tf_op jit(solution)/shard_map/ppermute | solution.py:608
  93.2 5.4 %collective-permute-start.6 = (bf16[96,2432]{1,0:T(8,128)(2,1)}, bf16[96,2432]{1,0:T(8,128)(2,1)}, u32[]{:S(2)}, u32[]{:S(2)}) collective-permute-start(bf16[96,2432]{1,0:T(8,128)(2,1)} %collective-permute-done.5.refs_6_), channel_id=1, source_target_pairs={{0,1},{1,0},{2,3},{3,2},{4,5},{5,4},{6,7},{7,6},{8,9},{9,8},{10,11... | collective-permute-start | bytes 1400840 | tf_op jit(solution)/shard_map/ppermute | solution.py:608
  93.6 3.2 copy-start.12
  93.6 1.8 collective-permute-start.11
  95.4 3.2 copy-start.13
  95.4 1.4 collective-permute-start.13
  96.8 1.8 copy-start.14
  96.8 1.7 collective-permute-start.9
  122.7 34.1 %copy-start = (bf16[8,192,896]{2,1,0:T(8,128)(2,1)}, bf16[8,192,896]{2,1,0:T(8,128)(2,1)S(1)}, u32[]{:S(2)}) copy-start(bf16[8,192,896]{2,1,0:T(8,128)(2,1)S(1)} %all-to-all-done.1) | copy-start | bytes 8257540
  225.7 33.0 %all-to-all-start.2 = ((bf16[8,192,768]{2,1,0:T(8,128)(2,1)}), bf16[8,192,768]{2,1,0:T(8,128)(2,1)S(1)}, u32[]{:S(2)}, u32[]{:S(2)}) async-start(bf16[8,192,768]{2,1,0:T(8,128)(2,1)} %bitcast.60), calls=%async_computation.2 | async-start | bytes 4718592 | tf_op jit(solution)/shard_map/all_to_all | solution.py:685
  258.7 1.4 copy-start.3
  260.2 33.8 %all-to-all-start.3 = ((bf16[8,192,768]{2,1,0:T(8,128)(2,1)}), bf16[8,192,768]{2,1,0:T(8,128)(2,1)}, u32[]{:S(2)}, u32[]{:S(2)}) async-start(bf16[8,192,768]{2,1,0:T(8,128)(2,1)} %bitcast.56), calls=%async_computation.3 | async-start | bytes 4718592 | tf_op jit(solution)/shard_map/all_to_all | solution.py:685
  265.9 209.3 %reduce-scatter.5.cloned.1.call-start = ((), (), s32[]{:S(2)}) async-start(), calls=%async_computation.7 | async-start | bytes 7864320 | tf_op jit(solution)/shard_map/reduce_scatter | solution.py:708
  333.9 4.9 collective-permute-start.14
  344.2 17.7 %collective-permute-start.15 = (bf16[96,3200]{1,0:T(8,128)(2,1)S(1)}, bf16[96,3200]{1,0:T(8,128)(2,1)S(1)}, u32[]{:S(2)}, u32[]{:S(2)}) collective-permute-start(bf16[96,3200]{1,0:T(8,128)(2,1)S(1)} %get-tuple-element.138), channel_id=1, source_target_pairs={{0,6},{1,7},{2,4},{3,5},{4,2},{5,3},{6,0},{7,1},{8,14},{9,15},{10,... | collective-permute-start | bytes 1843208 | tf_op jit(solution)/shard_map/ppermute | solution.py:608
  345.7 28.6 %collective-permute-start.16 = (bf16[96,3200]{1,0:T(8,128)(2,1)S(1)}, bf16[96,3200]{1,0:T(8,128)(2,1)S(1)}, u32[]{:S(2)}, u32[]{:S(2)}) collective-permute-start(bf16[96,3200]{1,0:T(8,128)(2,1)S(1)} %get-tuple-element.140), channel_id=1, source_target_pairs={{0,2},{1,3},{2,0},{3,1},{4,6},{5,7},{6,4},{7,5},{8,10},{9,11},{10,... | collective-permute-start | bytes 1843208 | tf_op jit(solution)/shard_map/ppermute | solution.py:608
  347.2 27.1 %collective-permute-start.17 = (bf16[96,3200]{1,0:T(8,128)(2,1)S(1)}, bf16[96,3200]{1,0:T(8,128)(2,1)}, u32[]{:S(2)}, u32[]{:S(2)}) collective-permute-start(bf16[96,3200]{1,0:T(8,128)(2,1)S(1)} %get-tuple-element.139), channel_id=1, source_target_pairs={{0,4},{1,5},{2,6},{3,7},{4,0},{5,1},{6,2},{7,3},{8,12},{9,13},{10,... | collective-permute-start | bytes 1843208 | tf_op jit(solution)/shard_map/ppermute | solution.py:608
  376.1 16.8 %collective-permute-start.18 = (bf16[96,3200]{1,0:T(8,128)(2,1)S(1)}, bf16[96,3200]{1,0:T(8,128)(2,1)S(1)}, u32[]{:S(2)}, u32[]{:S(2)}) collective-permute-start(bf16[96,3200]{1,0:T(8,128)(2,1)S(1)} %fusion.8), channel_id=1, source_target_pairs={{0,8},{1,9},{2,10},{3,11},{4,12},{5,13},{6,14},{7,15}} | collective-permute-start | bytes 1843208 | tf_op jit(solution)/shard_map/ppermute | solution.py:625
  379.6 14.1 %collective-permute-start.19 = (bf16[96,3200]{1,0:T(8,128)(2,1)S(1)}, bf16[96,3200]{1,0:T(8,128)(2,1)S(1)}, u32[]{:S(2)}, u32[]{:S(2)}) collective-permute-start(bf16[96,3200]{1,0:T(8,128)(2,1)S(1)} %fusion.8), channel_id=1, source_target_pairs={{24,16},{25,17},{26,18},{27,19},{28,20},{29,21},{30,22},{31,23}} | collective-permute-start | bytes 1843208 | tf_op jit(solution)/shard_map/ppermute | solution.py:626
  393.0 6.5 %copy-start.5 = (f32[12,32]{1,0:T(8,128)S(1)}, f32[12,32]{1,0:T(8,128)}, u32[]{:S(2)}) copy-start(f32[12,32]{1,0:T(8,128)} %get-tuple-element.89) | copy-start | bytes 4612
  393.0 0.7 collective-permute-start.20
  393.8 4.5 copy-start.1
  393.8 4.4 copy-start.2
  395.0 2.2 collective-permute-start.21
  395.7 74.3 %collective-permute-start.22 = (bf16[96,3200]{1,0:T(8,128)(2,1)}, bf16[96,3200]{1,0:T(8,128)(2,1)}, u32[]{:S(2)}, u32[]{:S(2)}) collective-permute-start(bf16[96,3200]{1,0:T(8,128)(2,1)} %get-tuple-element.141), channel_id=1, source_target_pairs={{16,24},{17,25},{18,26},{19,27},{20,28},{21,29},{22,30},{23,31}} | collective-permute-start | bytes 1843208 | tf_op jit(solution)/shard_map/ppermute | solution.py:625
  398.2 71.7 %collective-permute-start.23 = (bf16[96,3200]{1,0:T(8,128)(2,1)}, bf16[96,3200]{1,0:T(8,128)(2,1)}, u32[]{:S(2)}, u32[]{:S(2)}) collective-permute-start(bf16[96,3200]{1,0:T(8,128)(2,1)} %fusion.5), channel_id=1, source_target_pairs={{8,0},{9,1},{10,2},{11,3},{12,4},{13,5},{14,6},{15,7}} | collective-permute-start | bytes 1843208 | tf_op jit(solution)/shard_map/ppermute | solution.py:626
Sparse Core Ops, SparseCore 0:
  179.0 60.6 reduce-scatter.2
  269.0 111.9 reduce-scatter.4

commit v2 on v1

--- a/solution.py
+++ b/solution.py
@@ -157,9 +157,8 @@
     blocks, experts, me_ref, tokens_ref, table_ref, slot_row_ref, *refs,
 ):
     w_in = refs[:blocks]
-    p_in = refs[blocks : 2 * blocks]
     (q_ref, k_ref, v_ref, lse_ref, att_ref, res_ref, n1_ref, n2_ref, logit_ref, sent_ref,
-     qkv_ref, proj_ref, small_ref, small_t_ref) = refs[2 * blocks :]
+     small_ref, small_t_ref, qkv_ref, proj_ref) = refs[blocks:]
     step = pl.program_id(0)
     last = pl.num_programs(0) - 1
     seq, width = tokens_ref.shape
@@ -172,8 +171,8 @@
         for j in range(blocks):
             start = pl.multiple_of((me ^ j) * rows, rows) if blocks > 1 else 0
             qkv_ref[pl.ds(start, rows), :] = w_in[j][:, : 3 * width]
-            small_ref[pl.ds(start, rows), :] = w_in[j][:, 3 * width :]
-            proj_ref[pl.ds(start, rows), :] = p_in[j][...]
+            proj_ref[pl.ds(start, rows), :] = w_in[j][:, 3 * width : 4 * width]
+            small_ref[pl.ds(start, rows), :] = w_in[j][:, 4 * width :]
         small_t_ref[...] = small_ref[...].astype(F32).T
         x = tokens_ref[...].astype(F32)
         r = lax.rsqrt(jnp.mean(x * x, axis=-1, keepdims=True) + EPS)
@@ -226,7 +225,7 @@
             sent_ref[e * per : (e + 1) * per, :] = dot(hit.astype(BF16), n2).astype(BF16)
 
 
-def front(me, tokens, table, slot_row, w_blocks, p_blocks, experts, slots):
+def front(me, tokens, table, slot_row, w_blocks, experts, slots):
     seq, width = tokens.shape
     blocks = len(w_blocks)
     groups = width // GROUP
@@ -239,8 +238,7 @@
             sds((seq, LANES), F32), sds((seq, width), BF16), sds((seq, width), F32),
             sds((seq, width), BF16), sds((seq, width), BF16), sds((seq, LANES), F32),
             sds((slots, width), BF16),
-            sds((width, 3 * width), BF16), sds((width, width), BF16), sds((width, LANES), BF16),
-            sds((LANES, width), F32),
+            sds((width, LANES), BF16), sds((LANES, width), F32),
         ],
         grid=(groups,),
         in_specs=[
@@ -248,20 +246,41 @@
             pl.BlockSpec((per_group, seq, seq), lambda g: (g, 0, 0)),
             whole((8, seq)),
         ]
-        + [whole(b.shape) for b in w_blocks]
-        + [whole(b.shape) for b in p_blocks],
+        + [whole(b.shape) for b in w_blocks],
         out_specs=[
             col, col, col,
             whole((seq, LANES)), whole((seq, width)), whole((seq, width)),
             whole((seq, width)), whole((seq, width)), whole((seq, LANES)),
             whole((slots, width)),
-            whole((width, 3 * width)), whole((width, width)), whole((width, LANES)),
-            whole((LANES, width)),
+            whole((width, LANES)), whole((LANES, width)),
         ],
+        scratch_shapes=[pltpu.VMEM((width, 3 * width), BF16), pltpu.VMEM((width, width), BF16)],
         flops=2 * seq * width * width * 4 + 2 * slots * seq * width + 8 * seq * seq * width,
         moved=30_000_000,
         name="front",
-    )(me, tokens, table, slot_row, *w_blocks, *p_blocks)
+    )(me, tokens, table, slot_row, *w_blocks)
+
+
+def assemble_kernel(blocks, me_ref, *refs):
+    qkv_ref, proj_ref = refs[-2:]
+    wide = qkv_ref.shape[1]
+    high = proj_ref.shape[1]
+    for j in range(blocks):
+        rows = refs[j].shape[0]
+        start = pl.multiple_of((me_ref[0] ^ j) * rows, rows) if blocks > 1 else 0
+        qkv_ref[pl.ds(start, rows), :] = refs[j][:, :wide]
+        proj_ref[pl.ds(start, rows), :] = refs[j][:, wide : wide + high]
+
+
+def assemble(me, w_blocks, width):
+    return call(
+        functools.partial(assemble_kernel, len(w_blocks)),
+        [sds((width, 3 * width), BF16), sds((width, width), BF16)],
+        grid=(1,),
+        in_specs=[smem()] + [whole(b.shape) for b in w_blocks],
+        out_specs=[whole((width, 3 * width)), whole((width, width))],
+        name="assemble",
+    )(me, *w_blocks)
 
 
 def gelu_parts(v):
@@ -280,10 +299,10 @@
 def expert_kernel(first, ranks, tile, *refs):
     if first:
         (me_ref, rows_ref, cotx_ref, small_ref, win_ref, wout_ref,
-         act_ref, gp_ref, buf_ref, rows_t, sg_ref, sg_t) = refs
+         act_ref, gp_ref, d_ref, buf_ref, rows_t, sg_ref, sg_t) = refs
     else:
         (rows_ref, sg_ref, rows_t, sg_t, win_ref, wout_ref, _a, _g,
-         act_ref, gp_ref, buf_ref) = refs
+         act_ref, gp_ref, d_ref, buf_ref) = refs
     step = pl.program_id(0)
     total, width = rows_ref.shape
     if first:
@@ -305,6 +324,10 @@
             rows_t[...] = rows_ref[...].T
             sg_t[...] = sg_ref[...].T
 
+    @pl.when(step == 0)
+    def _():
+        d_ref[...] = jnp.zeros_like(d_ref)
+
     w1 = win_ref[...]
     w2 = wout_ref[...]
     for at in range(0, total, tile):
@@ -312,8 +335,10 @@
         pre = dot(rows_ref[here, :], w1)
         ga = dot_nt(sg_ref[here, :], w2)
         act, slope = gelu_parts(pre)
-        act_ref[here, :] = act.astype(BF16)
+        low = act.astype(BF16)
+        act_ref[here, :] = low
         gp_ref[here, :] = (ga * slope).astype(BF16)
+        d_ref[here, :] += jnp.sum(low.astype(F32) * ga, axis=1, keepdims=True)
     block = w1.shape[1]
     part = width // ranks
     gwin = dot(rows_t[...], gp_ref[...]).astype(BF16)
@@ -331,13 +356,13 @@
             ]
 
 
-def expert_chunk(first, ins, chunk, ranks, total, width, hidden):
-    start, count = chunk
+def expert_chunk(first, ins, start, count, ranks, total, width, hidden):
     block = 256
     per_rank = hidden // ranks // block
     part = width // ranks
     piece = block // ranks
     high = part + (width // block) * piece
+    wide = ranks * block
 
     def at(s):
         return lax.rem(s, ranks) * per_rank + start + lax.div(s, ranks)
@@ -345,12 +370,9 @@
     win_spec = pl.BlockSpec((width, block), lambda s: (0, at(s)))
     wout_spec = pl.BlockSpec((block, width), lambda s: (at(s), 0))
     col = pl.BlockSpec((total, block), lambda s: (0, at(s)))
-    outs = [
-        sds((total, hidden), BF16),
-        sds((total, hidden), BF16),
-        sds((ranks, count, high, ranks * block), BF16),
-    ]
-    out_specs = [col, col, whole((ranks, count, high, ranks * block))]
+    buf = (ranks, count, high, wide)
+    outs = [sds((total, hidden), BF16), sds((total, hidden), BF16), sds((total, LANES), F32), sds(buf, BF16)]
+    out_specs = [col, col, whole((total, LANES)), whole(buf)]
     kw = {}
     if first:
         in_specs = [smem(), whole((total, width)), whole((total, width + LANES)), whole((width, LANES)), win_spec, wout_spec]
@@ -376,27 +398,42 @@
     )(*ins)
 
 
-def rows_kernel(transposed, a_ref, w_ref, o_ref):
-    prod = dot_nt if transposed else dot
-    o_ref[...] = prod(a_ref[...], w_ref[...]).astype(BF16)
-
-
-def rows_out(transposed, a, w, width):
+def rows_out_kernel(a_ref, w_ref, o_ref):
+    o_ref[...] = dot(a_ref[...], w_ref[...]).astype(BF16)
+
+
+def rows_back_kernel(a_ref, w_ref, *refs):
+    o_ref = refs[-1]
+    width = w_ref.shape[0]
+    o_ref[:, :width] = dot_nt(a_ref[...], w_ref[...]).astype(BF16)
+    d = refs[0][...]
+    for other in refs[1:-1]:
+        d = d + other[...]
+    high = d.astype(BF16)
+    low = (d - high.astype(F32)).astype(BF16)
+    lane = iota(d.shape, 1)
+    zero = jnp.zeros_like(d)
+    o_ref[:, width:] = jnp.where(lane == 0, high.astype(F32), jnp.where(lane == 1, low.astype(F32), zero)).astype(BF16)
+
+
+def rows_product(kernel, a, w, wide, extra, name):
     total, hidden = a.shape
-    tile = total // 8
-    return call(
-        functools.partial(rows_kernel, transposed),
-        sds((total, width), BF16),
-        grid=(8,),
-        in_specs=[pl.BlockSpec((tile, hidden), lambda i: (i, 0)), whole(w.shape)],
-        out_specs=pl.BlockSpec((tile, width), lambda i: (i, 0)),
-        flops=2 * total * hidden * width,
-        moved=2 * (total * hidden + hidden * width + total * width),
-        name="expert_rows_back" if transposed else "expert_rows_out",
-    )(a, w)
-
-
-def norm_back(x, grad, gain, count):
+    steps = 3
+    tile = total // steps
+    return call(
+        kernel,
+        sds((total, wide), BF16),
+        grid=(steps,),
+        in_specs=[pl.BlockSpec((tile, hidden), lambda i: (i, 0)), whole(w.shape)]
+        + [pl.BlockSpec((tile, LANES), lambda i: (i, 0))] * len(extra),
+        out_specs=pl.BlockSpec((tile, wide), lambda i: (i, 0)),
+        flops=2 * total * hidden * wide,
+        moved=2 * (total * hidden + hidden * wide + total * wide),
+        name=name,
+    )(a, w, *extra)
+
+
+def norm_back(x, grad, gain):
     r = lax.rsqrt(jnp.mean(x * x, axis=-1, keepdims=True) + EPS)
     u = grad * gain
     inner = jnp.mean(u * x, axis=-1, keepdims=True)
@@ -404,86 +441,92 @@
     return r * u - (r * r * r) * x * inner, jnp.sum(grad * xr, axis=0, keepdims=True)
 
 
-def mid_kernel(
-    experts, ret_ref, back_ref, slot_ref, res_ref, logit_ref, cot_ref, n2_ref, att_ref,
-    proj_ref, small_ref, small_t_ref, out_ref, gres_ref, gatt_ref, gproj_ref, gsmall_ref,
-):
-    seq, width = res_ref.shape
-    slots = ret_ref.shape[0]
-    lane = iota((seq, LANES), 1)
-    spot = iota((seq, slots), 1)
-    s0 = slot_ref[:, 0:1].astype(jnp.int32)
-    s1 = slot_ref[:, 1:2].astype(jnp.int32)
-    h0 = (spot == s0).astype(BF16)
-    h1 = (spot == s1).astype(BF16)
+def pair_gates(slot_ref, logit_ref):
+    logits = logit_ref[...]
+    lane = iota(logits.shape, 1)
     hot0 = lane == slot_ref[:, 2:3].astype(jnp.int32)
     hot1 = lane == slot_ref[:, 3:4].astype(jnp.int32)
-    logits = logit_ref[...]
     c0 = jnp.sum(jnp.where(hot0, logits, 0.0), axis=1, keepdims=True)
     c1 = jnp.sum(jnp.where(hot1, logits, 0.0), axis=1, keepdims=True)
     top = jnp.maximum(c0, c1)
     e0, e1 = jnp.exp(c0 - top), jnp.exp(c1 - top)
-    g0, g1 = e0 / (e0 + e1), e1 / (e0 + e1)
-    cot = cot_ref[...].astype(F32)
+    return e0 / (e0 + e1), e1 / (e0 + e1), hot0, hot1
+
+
+def pair_hits(slot_ref, slots):
+    spot = iota((slot_ref.shape[0], slots), 1)
+    h0 = (spot == slot_ref[:, 0:1].astype(jnp.int32)).astype(BF16)
+    h1 = (spot == slot_ref[:, 1:2].astype(jnp.int32)).astype(BF16)
+    return h0, h1
+
+
+def output_kernel(ret_ref, slot_ref, res_ref, logit_ref, out_ref):
+    h0, h1 = pair_hits(slot_ref, ret_ref.shape[0])
+    g0, g1, _, _ = pair_gates(slot_ref, logit_ref)
     ret = ret_ref[...]
-    p0 = dot(h0, ret)
-    p1 = dot(h1, ret)
+    out_ref[...] = (res_ref[...] + (g0 * dot(h0, ret) + g1 * dot(h1, ret))).astype(BF16)
+
+
+def output_rows(returned, slot_col, res, logits):
+    ins = (returned, slot_col, res, logits)
+    return call(
+        output_kernel,
+        sds(res.shape, BF16),
+        grid=(1,),
+        in_specs=[whole(x.shape) for x in ins],
+        out_specs=whole(res.shape),
+        flops=4 * returned.shape[0] * res.size,
+        moved=6_000_000,
+        name="output_rows",
+    )(*ins)
+
+
+def mid_kernel(
+    experts, back_ref, slot_ref, res_ref, logit_ref, cot_ref, n2_ref, att_ref,
+    proj_ref, small_ref, small_t_ref, gres_ref, gatt_ref, gpack_ref,
+):
+    seq, width = res_ref.shape
+    h0, h1 = pair_hits(slot_ref, back_ref.shape[0])
+    g0, g1, hot0, hot1 = pair_gates(slot_ref, logit_ref)
+    back = back_ref[:, :width]
+    sides = back_ref[:, width:]
+    d0 = jnp.sum(dot(h0, sides), axis=1, keepdims=True)
+    d1 = jnp.sum(dot(h1, sides), axis=1, keepdims=True)
+    glog = jnp.where(hot0, d0 - g0 * (d0 + d1), 0.0) + jnp.where(hot1, d1 - g1 * (d0 + d1), 0.0)
+    glog = glog.astype(BF16)
     x = res_ref[...]
-    out_ref[...] = (x + (g0 * p0 + g1 * p1)).astype(BF16)
-    d0 = jnp.sum(cot * p0, axis=1, keepdims=True)
-    d1 = jnp.sum(cot * p1, axis=1, keepdims=True)
-    mean = g0 * d0 + g1 * d1
-    glog = jnp.where(hot0, g0 * (d0 - mean), 0.0) + jnp.where(hot1, g1 * (d1 - mean), 0.0)
-    glog = glog.astype(BF16)
-    grad = dot(h0 + h1, back_ref[...]) + dot_nt(glog, jnp.where(iota((width, LANES), 1) < experts, small_ref[...], jnp.zeros_like(small_ref[...])))
-    gx, ggain = norm_back(x, grad, small_t_ref[experts + 1 : experts + 2, :], width)
-    gres = gx + cot
+    small = small_ref[...]
+    router = jnp.where(iota((width, LANES), 1) < experts, small, jnp.zeros_like(small))
+    grad = dot(h0 + h1, back) + dot_nt(glog, router)
+    gx, ggain = norm_back(x, grad, small_t_ref[experts + 1 : experts + 2, :])
+    gres = gx + cot_ref[...].astype(F32)
     gres_ref[...] = gres
     branch = gres.astype(BF16)
-    gproj_ref[...] = dot_tn(att_ref[...], branch).astype(BF16)
     gatt_ref[...] = dot_nt(branch, proj_ref[...]).astype(BF16)
+    gpack_ref[:, :width] = dot_tn(att_ref[...], branch).astype(BF16)
     gain_rows = jnp.where(iota((LANES, width), 0) == experts + 1, ggain, 0.0)
-    gsmall_ref[...] = dot_tn(n2_ref[...], glog) + gain_rows.T
-
-
-def mid(experts, returned, back, slot_col, res, logits, cot, n2, att, proj, small, small_t):
+    gpack_ref[:, width:] = (dot_tn(n2_ref[...], glog) + gain_rows.T).astype(BF16)
+
+
+def mid(experts, back, slot_col, res, logits, cot, n2, att, proj, small, small_t):
     seq, width = res.shape
-    ins = (returned, back, slot_col, res, logits, cot, n2, att, proj, small, small_t)
+    ins = (back, slot_col, res, logits, cot, n2, att, proj, small, small_t)
     return call(
         functools.partial(mid_kernel, experts),
-        [
-            sds((seq, width), BF16), sds((seq, width), F32), sds((seq, width), BF16),
-            sds((width, width), BF16), sds((width, LANES), F32),
-        ],
+        [sds((seq, width), F32), sds((seq, width), BF16), sds((width, width + LANES), BF16)],
         in_specs=[whole(a.shape) for a in ins],
-        out_specs=[
-            whole((seq, width)), whole((seq, width)), whole((seq, width)),
-            whole((width, width)), whole((width, LANES)),
-        ],
+        out_specs=[whole((seq, width)), whole((seq, width)), whole((width, width + LANES))],
         grid=(1,),
-        flops=6 * returned.shape[0] * seq * width + 4 * seq * width * width,
-        moved=15_000_000,
+        flops=2 * back.shape[0] * seq * width + 4 * seq * width * width,
+        moved=12_000_000,
         name="token_side",
     )(*ins)
 
 
-def tail_kernel(
-    experts, buckets, tokens_ref, table_ref, q_ref, k_ref, v_ref, gatt_ref, lse_ref, n1_ref, gres_ref,
-    wq_ref, wk_ref, wv_ref, small_t_ref, rev_ref, gproj_ref, gsmall_ref,
-    pack_ref, gtok_ref, gbias_ref, acc_scr, diag_scr, g_scr, n1t_scr,
-):
-    step = pl.program_id(0)
-    last = pl.num_programs(0) - 1
-    seq, width = tokens_ref.shape
+def heads_back(group, table_ref, q_ref, k_ref, v_ref, gatt_ref, lse_ref, g_scr, diag_ref):
+    seq = q_ref.shape[0]
     half = seq // 2
     scale = HEAD_DIM ** (-0.5)
-
-    @pl.when(step == 0)
-    def _():
-        acc_scr[...] = jnp.zeros_like(acc_scr)
-        diag_scr[...] = jnp.zeros_like(diag_scr)
-        n1t_scr[...] = n1_ref[...].T
-
     lane = iota((half, LANES), 1)
     full_lane = iota((seq, LANES), 1)
     for pair in range(GROUP // LANES):
@@ -501,8 +544,8 @@
             dq = []
             for parity in range(2):
                 mine = (lane // HEAD_DIM) == parity
-                head = step * (GROUP // HEAD_DIM) + 2 * pair + parity
-                level = jnp.sum(jnp.where(lane == head, lse_ref[qrows, :], 0.0), axis=1, keepdims=True)
+                head = group * (GROUP // HEAD_DIM) + 2 * pair + parity
+                level = lse_ref[qrows, head : head + 1]
                 qm = jnp.where(mine, qp, jnp.zeros_like(qp))
                 gm = jnp.where(mine, gp, jnp.zeros_like(gp))
                 s = dot_nt(qm, kp) * scale + table_ref[2 * pair + parity, qrows, :span]
@@ -536,118 +579,181 @@
             acc = skew[parity][0:8, :]
             for i in range(1, LANES // 8):
                 acc = acc + pltpu.roll(skew[parity][i * 8 : (i + 1) * 8, :], seq - i * 8, 1)
-            head = step * (GROUP // HEAD_DIM) + 2 * pair + parity
-            diag_scr[pl.ds(pl.multiple_of(head * 8, 8), 8), :] = acc
-
-    base = pl.multiple_of(step * GROUP, GROUP)
-    w_refs = (wq_ref, wk_ref, wv_ref)
-    n1t = n1t_scr[...]
-    for i in range(3):
+            at = 8 * (2 * pair + parity)
+            diag_ref[at : at + 8, :] = acc
+
+
+def tail_kernel(group, *refs):
+    (table_ref, q_ref, k_ref, v_ref, gatt_ref, lse_ref, n1_ref, wq_ref, wk_ref, wv_ref) = refs[:10]
+    acc_in = refs[10] if group else None
+    pack_ref, acc_ref, diag_ref, g_scr = refs[-4:]
+    heads_back(group, table_ref, q_ref, k_ref, v_ref, gatt_ref, lse_ref, g_scr, diag_ref)
+    acc = acc_in[...] if group else None
+    for i, w_ref in enumerate((wq_ref, wk_ref, wv_ref)):
         g = g_scr[i]
-        at = pl.multiple_of(i * width + base, GROUP)
-        pack_ref[:, pl.ds(at, GROUP)] = dot(n1t, g).astype(BF16)
-        acc_scr[...] += dot_nt(g, w_refs[i][...])
-
-    @pl.when(step == last)
-    def _():
-        x = tokens_ref[...].astype(F32)
-        gx, ggain = norm_back(x, acc_scr[...], small_t_ref[experts : experts + 1, :], width)
-        gtok_ref[...] = (gx + gres_ref[...]).astype(BF16)
-        gain_rows = jnp.where(iota((LANES, width), 0) == experts, ggain, 0.0)
-        pack_ref[:, 3 * width : 4 * width] = gproj_ref[...]
-        pack_ref[:, 4 * width :] = (gsmall_ref[...] + gain_rows.T).astype(BF16)
-        count = diag_scr.shape[0]
-        place = lax.rem(iota((count, seq), 0), 8)
-        diag = diag_scr[...]
-        total = jnp.where(place == 0, diag, 0.0)
-        for r in range(1, 8):
-            total = total + jnp.where(place == r, pltpu.roll(diag, seq - r, 1), 0.0)
-        hot = (iota((buckets, seq), 0) == rev_ref[...]).astype(F32)
-        per_row = lax.dot_general(
-            total, hot, (((1,), (1,)), ((), ())), precision=lax.Precision.HIGHEST, preferred_element_type=F32
-        )
-        gbias_ref[...] = jnp.sum(per_row.reshape(count // 8, 8, buckets), axis=1)
-
-
-def tail(experts, buckets, tokens, table, q, k, v, gatt, lse, n1, gres, qkv, small_t, rev_buckets, gproj, gsmall):
-    seq, width = tokens.shape
-    heads = table.shape[0]
+        pack_ref[:, i * GROUP : (i + 1) * GROUP] = dot_tn(n1_ref[...], g).astype(BF16)
+        more = dot_nt(g, w_ref[...])
+        acc = more if acc is None else acc + more
+    acc_ref[...] = acc
+
+
+def tail(group, table, q, k, v, gatt, lse, n1, qkv, acc):
+    seq, width = n1.shape
     groups = width // GROUP
     per_group = GROUP // HEAD_DIM
-    col = pl.BlockSpec((seq, GROUP), lambda g: (0, g))
+    col = pl.BlockSpec((seq, GROUP), lambda _: (0, group))
 
     def wcol(i):
-        return pl.BlockSpec((width, GROUP), lambda g: (0, i * groups + g))
-
-    return call(
-        functools.partial(tail_kernel, experts, buckets),
-        [sds((width, 4 * width + LANES), BF16), sds((seq, width), BF16), sds((heads, buckets), F32)],
-        grid=(groups,),
+        return pl.BlockSpec((width, GROUP), lambda _: (0, i * groups + group))
+
+    return call(
+        functools.partial(tail_kernel, group),
+        [sds((width, 3 * GROUP), BF16), sds((seq, width), F32), sds((8 * per_group, seq), F32)],
+        grid=(1,),
         in_specs=[
-            whole((seq, width)),
-            pl.BlockSpec((per_group, seq, seq), lambda g: (g, 0, 0)),
+            pl.BlockSpec((per_group, seq, seq), lambda _: (group, 0, 0)),
             col, col, col, col,
-            whole((seq, LANES)), whole((seq, width)), whole((seq, width)),
+            whole((seq, LANES)), whole((seq, width)),
             wcol(0), wcol(1), wcol(2),
-            whole((LANES, width)), whole((1, seq)), whole((width, width)), whole((width, LANES)),
-        ],
-        out_specs=[whole((width, 4 * width + LANES)), whole((seq, width)), whole((heads, buckets))],
-        scratch_shapes=[
-            pltpu.VMEM((seq, width), F32),
-            pltpu.VMEM((heads * 8, seq), F32),
-            pltpu.VMEM((3, seq, GROUP), BF16),
-            pltpu.VMEM((width, seq), BF16),
-        ],
-        flops=12 * seq * width * width + 20 * seq * seq * width,
-        moved=30_000_000,
+        ]
+        + [whole((seq, width))] * len(acc),
+        out_specs=[whole((width, 3 * GROUP)), whole((seq, width)), whole((8 * per_group, seq))],
+        scratch_shapes=[pltpu.VMEM((3, seq, GROUP), BF16)],
+        flops=4 * seq * width * width + 7 * seq * seq * width,
+        moved=10_000_000,
         name="tail",
-    )(tokens, table, q, k, v, gatt, lse, n1, gres, qkv, qkv, qkv, small_t, rev_buckets[None, :], gproj, gsmall)
+    )(table, q, k, v, gatt, lse, n1, qkv, qkv, qkv, *acc)
+
+
+def last_kernel(
+    experts, own_rows, parts, tokens_ref, gres_ref, acc_ref, small_t_ref, rev_ref, *refs,
+):
+    diag_refs = refs[:parts]
+    gtok_ref, small_ref = refs[parts:]
+    seq, width = tokens_ref.shape
+    x = tokens_ref[...].astype(F32)
+    gx, ggain = norm_back(x, acc_ref[...], small_t_ref[experts : experts + 1, :])
+    gtok_ref[...] = (gx + gres_ref[...]).astype(BF16)
+    gain_rows = jnp.where(iota((LANES, width), 0) == experts, ggain, 0.0)
+    diag = jnp.concatenate([d[...] for d in diag_refs], axis=0)
+    count = diag.shape[0]
+    place = lax.rem(iota((count, seq), 0), 8)
+    total = jnp.where(place == 0, diag, 0.0)
+    for r in range(1, 8):
+        total = total + jnp.where(place == r, pltpu.roll(diag, seq - r, 1), 0.0)
+    hot = (iota((LANES, seq), 0) - (experts + 2) == rev_ref[...]).astype(F32)
+    per_row = lax.dot_general(
+        total, hot, (((1,), (1,)), ((), ())), precision=lax.Precision.HIGHEST, preferred_element_type=F32
+    )
+    copies = (lax.rem(iota((width, count), 0), own_rows) == lax.div(iota((width, count), 1), 8)).astype(F32)
+    spread = jnp.dot(copies, per_row, precision=lax.Precision.HIGHEST, preferred_element_type=F32)
+    small_ref[...] = (gain_rows.T + spread).astype(BF16)
+
+
+def last(experts, own_rows, tokens, gres, acc, small_t, rev_buckets, diags):
+    seq, width = tokens.shape
+    ins = (tokens, gres, acc, small_t, rev_buckets[None, :], *diags)
+    return call(
+        functools.partial(last_kernel, experts, own_rows, len(diags)),
+        [sds((seq, width), BF16), sds((width, LANES), BF16)],
+        grid=(1,),
+        in_specs=[whole(x.shape) for x in ins],
+        out_specs=[whole((seq, width)), whole((width, LANES))],
+        moved=5_000_000,
+        name="last",
+    )(*ins)
 
 
 def swap(value, mask, size):
     return lax.ppermute(value, "shard", [(i, i ^ mask) for i in range(size)])
 
 
-def gather_blocks(value, size):
+def gather_blocks(value, size, beside):
     if size != 8:
-        return [lax.all_gather(value, "shard", axis=0, tiled=True)]
-    far = {j: swap(value, j, size) for j in (6, 2, 4)}
-    far[0] = value
-    near = {j ^ 1: swap(far[j], 1, size) for j in (0, 6, 2, 4)}
-    return [far[j] if j in far else near[j] for j in range(8)]
-
-
-def line_total(value, ranks):
-    own = value.astype(F32)
-    right = left = value
-    gained = own
-    for t in range(1, ranks):
-        a = lax.ppermute(right, "rep", [(t - 1, t)])
-        b = lax.ppermute(left, "rep", [(ranks - t, ranks - 1 - t)])
-        gained = gained + (a.astype(F32) + b.astype(F32))
-        right = (own + a.astype(F32)).astype(BF16)
-        left = (own + b.astype(F32)).astype(BF16)
-    return gained
-
-
-def reduce_small(pack, me, size, ranks):
+        return [lax.all_gather(value, "shard", axis=0, tiled=True)], beside
+    one, six, two, four = (swap(value, j, size) for j in (1, 6, 2, 4))
+    one, six, two, four, *beside = lax.optimization_barrier((one, six, two, four, *beside))
+    far = {0: value, 1: one, 6: six, 2: two, 4: four}
+    near = {j ^ 1: swap(far[j], 1, size) for j in (6, 2, 4)}
+    return [far[j] if j in far else near[j] for j in range(8)], beside
+
+
+def tie(*values):
+    return lax.optimization_barrier(values)
+
+
+def inward(value):
+    return lax.ppermute(value, "rep", [(0, 1), (3, 2)])
+
+
+def across(value):
+    return lax.ppermute(value, "rep", [(1, 2), (2, 1)])
+
+
+def outward(value):
+    return lax.ppermute(value, "rep", [(1, 0), (2, 3)])
+
+
+def add(*values):
+    total = values[0].astype(F32)
+    for value in values[1:]:
+        total = total + value.astype(F32)
+    return total.astype(BF16)
+
+
+def line_total(value, at_end):
+    near = add(value, inward(value))
+    total = add(near, across(near))
+    return jnp.where(at_end, outward(total), total)
+
+
+def finish_kernel(width, src_ref, *refs):
+    in_ref, out_ref = refs[-2:]
+    total = src_ref[0].astype(F32)
+    part, block = in_ref.shape
+    piece = out_ref.shape[0]
+    in_ref[...] = total[:part, :]
+    for j in range(width // block):
+        out_ref[:, j * block : (j + 1) * block] = total[part + j * piece : part + (j + 1) * piece, :]
+
+
+def finish(src, start, earlier, width, hidden, ranks):
+    count, high, wide = src.shape
+    block = wide // ranks
+    part = width // ranks
+    piece = block // ranks
+    per_rank = hidden // ranks // block
+    return call(
+        functools.partial(finish_kernel, width),
+        [sds((part, hidden), F32), sds((hidden // ranks, width), F32)],
+        grid=(count, ranks),
+        in_specs=[pl.BlockSpec((1, high, block), lambda c, r: (c, 0, r))]
+        + [pl.BlockSpec(memory_space=pl.ANY)] * len(earlier),
+        out_specs=[
+            pl.BlockSpec((part, block), lambda c, r: (0, r * per_rank + start + c)),
+            pl.BlockSpec((piece, width), lambda c, r: ((start + c) * ranks + r, 0)),
+        ],
+        input_output_aliases={1: 0, 2: 1} if earlier else {},
+        name="finish",
+    )(src, *earlier)
+
+
+def chip_sum(pack, me, size):
     if size != 8:
-        owned = lax.psum_scatter(pack, "shard", scatter_dimension=0, tiled=True)
-        return line_total(owned, ranks)
-    rows = pack.shape[0] // size
-    blocks = pack.reshape(4, 2, rows, pack.shape[1])
+        return pack
+    blocks = pack.reshape(4, 2, pack.shape[0] // size, pack.shape[1])
     core = me % 2
-    chip = me // 2
     keep = lax.dynamic_index_in_dim(blocks, core, 1, keepdims=False)
     send = lax.dynamic_index_in_dim(blocks, 1 - core, 1, keepdims=False)
-    both = keep.astype(F32) + swap(send, 1, size).astype(F32)
-    low = both.astype(BF16)
-    got = [
-        swap(lax.dynamic_index_in_dim(low, chip ^ (j // 2), 0, keepdims=False), j, size).astype(F32)
-        for j in (6, 2, 4)
-    ]
-    owned = lax.dynamic_index_in_dim(both, chip, 0, keepdims=False) + got[0] + got[1] + got[2]
-    return line_total(owned.astype(BF16), ranks)
+    return add(keep, swap(send, 1, size))
+
+
+def group_sum(both, me, size):
+    if size != 8:
+        return lax.psum_scatter(both, "shard", scatter_dimension=0, tiled=True)
+    chip = me // 2
+    got = [swap(lax.dynamic_index_in_dim(both, chip ^ (j // 2), 0, keepdims=False), j, size) for j in (6, 2, 4)]
+    return add(lax.dynamic_index_in_dim(both, chip, 0, keepdims=False), *got)
 
 
 def body(
@@ -670,15 +776,16 @@
     small = jnp.concatenate(
         [router, attn_gain[:, None], moe_gain[:, None], jnp.zeros((own_rows, LANES - experts - 2), BF16)], axis=1
     )
-    w_blocks = gather_blocks(jnp.concatenate([qkv_weight, small], axis=1), size)
-    p_blocks = gather_blocks(proj_weight, size)
+    packed = jnp.concatenate([qkv_weight, proj_weight, small], axis=1)
     rev_buckets = jnp.roll(buckets[::-1], 1)
-    table, slot_row, slot_col, cot_slots = prep(
-        routes.T, segments, rev_buckets, rel_bias, cotangent, experts, capacity
+    w_blocks, (table, slot_row, slot_col, cot_slots) = gather_blocks(
+        packed, size, prep(routes.T, segments, rev_buckets, rel_bias, cotangent, experts, capacity)
     )
-    (q, k, v, lse, att, res, n1, n2, logits, sent, qkv_full, proj_full, small_full, small_t) = front(
-        me_arr, tokens, table, slot_row, w_blocks, p_blocks, experts, slots
+    (q, k, v, lse, att, res, n1, n2, logits, sent, small_full, small_t) = front(
+        me_arr, tokens, table, slot_row, w_blocks, experts, slots
     )
+    me_late, logits = tie(me_arr, logits)
+    qkv_full, proj_full = assemble(me_late, w_blocks, width)
 
     def exchange(value):
         wide = value.shape[1]
@@ -688,54 +795,74 @@
         return moved.reshape(slots, wide)
 
     cot_rows = exchange(cot_slots)
+    cot_rows, sent = tie(cot_rows, sent)
     rows = exchange(sent)
     win = expert_in[0]
     wout = expert_out[0]
+    rank = lax.axis_index("rep").astype(jnp.int32)
+    at_end = (rank == 0) | (rank == ranks - 1)
     per_rank = hidden // ranks // 256
-    act, gpre, buf0, rows_t, sg, sg_t = expert_chunk(
-        True, (me_arr, rows, cot_rows, small_full, win, wout), (0, 1), ranks, slots, width, hidden
-    )
-    act, gpre, buf1 = expert_chunk(
-        False, (rows, sg, rows_t, sg_t, win, wout, act, gpre), (1, per_rank - 1), ranks, slots, width, hidden
-    )
-    result = rows_out(False, act, wout, width)
-    returned = exchange(result)
-    grad_sent = rows_out(True, gpre, win, width)
-    back = exchange(grad_sent)
 
     def scatter(buf):
         count, high, wide = buf.shape[1:]
-        return lax.psum_scatter(
-            buf.reshape(ranks * count * high, wide), "rep", scatter_dimension=0, tiled=True
-        ).reshape(count, high, wide)
-
-    done = [scatter(buf0), scatter(buf1)]
-    output, gres, gatt, gproj, gsmall = mid(
-        experts, returned, back, slot_col, res, logits, cotangent, n2, att, proj_full, small_full, small_t
-    )
-    pack, grad_tokens, gbias = tail(
-        experts, bucket_count, tokens, table, q, k, v, gatt, lse, n1, gres, qkv_full, small_t,
-        rev_buckets, gproj, gsmall,
-    )
-    grad_rel_bias = lax.psum(gbias, ("rep", "shard")).T
-    owned = reduce_small(pack, me, size, ranks)
-
-    pieces = jnp.concatenate(done, axis=0).astype(F32)
-    part = width // ranks
-    gin = pieces[:, :part, :].reshape(per_rank, part, ranks, 256)
-    grad_in = gin.transpose(1, 2, 0, 3).reshape(1, part, hidden)
-    piece = 256 // ranks
-    gout = pieces[:, part:, :].reshape(per_rank, width // 256, piece, ranks, 256)
-    grad_out = gout.transpose(0, 3, 2, 1, 4).reshape(1, hidden // ranks, width)
+        moved = lax.psum_scatter(buf.reshape(ranks * count * high, wide), "rep", scatter_dimension=0, tiled=True)
+        return moved.reshape(count, high, wide)
+
+    def chunk_of(first, ins, start, count):
+        return expert_chunk(first, ins, start, count, ranks, slots, width, hidden)
+
+    qkv_full, proj_full, rows = tie(qkv_full, proj_full, rows)
+    act, gpre, d0, buf0, rows_t, sg, sg_t = chunk_of(True, (me_arr, rows, cot_rows, small_full, win, wout), 0, 1)
+    part0 = scatter(buf0)
+    act, gpre, d1, buf1 = chunk_of(False, (rows, sg, rows_t, sg_t, win, wout, act, gpre), 1, per_rank - 1)
+    grad_sent = rows_product(rows_back_kernel, gpre, win, width + LANES, (d0, d1), "expert_rows_back")
+    back = exchange(grad_sent)
+    act, part0 = tie(act, part0)
+    part1 = scatter(buf1)
+    result = rows_product(rows_out_kernel, act, wout, width, (), "expert_rows_out")
+    back, result = tie(back, result)
+    returned = exchange(result)
+    gres, gatt, gproj = mid(experts, back, slot_col, res, logits, cotangent, n2, att, proj_full, small_full, small_t)
+    groups = width // GROUP
+    packs, diags, acc = [], [], ()
+
+    def tail_of(group, gatt):
+        pack, total, diag = tail(group, table, q, k, v, gatt, lse, n1, qkv_full, acc)
+        packs.append(pack)
+        diags.append(diag)
+        return (total,)
+
+    acc = tail_of(0, gatt)
+    sum_a = chip_sum(gproj, me, size)
+    gatt, sum_a = tie(gatt, sum_a)
+    acc = tail_of(1, gatt)
+    owned_a = group_sum(sum_a, me, size)
+    sum_b = chip_sum(jnp.concatenate(packs, axis=1), me, size)
+    gatt, owned_a, returned, sum_b = tie(gatt, owned_a, returned, sum_b)
+    acc = tail_of(2, gatt)
+    grad_tokens, gsmall = last(experts, own_rows, tokens, gres, acc[0], small_t, rev_buckets, diags)
+    sum_c = chip_sum(jnp.concatenate(packs[2:] + [gsmall], axis=1), me, size)
+    owned_a = line_total(owned_a, at_end).astype(F32)
+    owned_b = line_total(group_sum(sum_b, me, size), at_end).astype(F32)
+    owned_c = line_total(group_sum(sum_c, me, size), at_end).astype(F32)
+    output = output_rows(returned, slot_col, res, logits)
+    done = finish(part0, 0, (), width, hidden, ranks)
+    done = finish(part1, 1, done, width, hidden, ranks)
+    grad_in, grad_out = done[0][None], done[1][None]
+    heads = rel_bias.shape[1]
+    small_at = 3 * GROUP
+    bias_at = small_at + experts + 2
+    by_group = jnp.concatenate([owned_b, owned_c[:, :small_at]], axis=1)
+    grad_qkv = by_group.reshape(own_rows, groups, 3, GROUP).transpose(0, 2, 1, 3).reshape(own_rows, 3 * width)
     return (
         output,
         grad_tokens,
-        owned[:, : 3 * width],
-        owned[:, 3 * width : 4 * width],
-        owned[:, 4 * width : 4 * width + experts],
-        owned[:, 4 * width + experts],
-        owned[:, 4 * width + experts + 1],
-        grad_rel_bias,
+        grad_qkv,
+        owned_a[:, :width],
+        owned_a[:, width : width + experts],
+        owned_c[:, small_at + experts],
+        owned_a[:, width + experts + 1],
+        owned_c[:heads, bias_at : bias_at + bucket_count].T,
         grad_in,
         grad_out,
     )

time: 513 us -> 382 us (0.74)
  blocking collectives: 105 us -> 0 us
  waiting for transfers between devices: 141 us -> 86.8 us
  Pallas kernels: 159 us -> 184 us
  starting transfers between devices: 37 us -> 55.1 us
  local copies, waits for them, and re-layouts: 33.1 us -> 23.2 us
    psum x1 -> x0, blocking collectives: 70.4 us -> none  [body(): grad_rel_bias = lax.psum(gbias, ('rep', 'shard')).T]
    ppermute x18 -> x19, waiting for transfers between devices: 89.6 us -> 22.6 us  [swap(): return lax.ppermute(value, 'shard', [(i, i ^ mask) for i in range(size)])]
    all_to_all x1 -> x0, blocking collectives: 34.1 us -> none  [exchange(): lax.all_to_all(value.reshape(size, slots // size, wide), 'shard', split_a...]
    pallas_call x4 -> x11, Pallas kernels: 68.1 us -> 92 us  [the longest x3 31.6 us: tail(): call(functools.partial(tail_kernel, group), [sds((width, 3 * GROUP), BF16...]
    ppermute x6 -> x9, starting transfers between devices: 8.44 us -> 18.1 us  [the longest x3 12.2 us: inward(): return lax.ppermute(value, 'rep', [(0, 1), (3, 2)])]
    reshape x4 -> x2, local copies, waits for them, and re-layouts: 11.6 us -> 1.99 us  [body(): by_group.reshape(own_rows, groups, 3, GROUP).transpose(0, 2, 1, 3)]
    reduce_scatter x2, waiting for transfers between devices: 0.01 us -> 7.59 us  [scatter(): lax.psum_scatter(buf.reshape(ranks * count * high, wide), 'rep', scatter_...]
    all_to_all x3 -> x4, starting transfers between devices: 15.2 us -> 21.4 us  [exchange(): lax.all_to_all(value.reshape(size, slots // size, wide), 'shard', split_a...]
  transfers between devices with their start and end apart: 29 -> 34, of which waited for: 11 -> 18; matrix products, arithmetic and copies ran while one was open for 4% -> 7% of each run, Pallas kernels for 25% -> 41%
where the time goes in v2:
time: 382 us; the launch traced here: 375 us
  Pallas kernels  184 us (48%)
  waiting for transfers between devices  86.8 us (23%)
  starting transfers between devices  55.1 us (14%)
  local copies, waits for them, and re-layouts  23.2 us (6%)
  between operations  14.9 us (4%)
  other arithmetic  10.5 us (3%)
    pallas_call x2, Pallas kernels, expert_chunk(): call(functools.partial(expert_kernel, first, ranks, 256), outs, grid=(cou...  58.1 us
    all_to_all x4, waiting for transfers between devices, exchange(): lax.all_to_all(value.reshape(size, slots // size, wide), 'shard', split_a...  40.8 us
    pallas_call x3, Pallas kernels, tail(): call(functools.partial(tail_kernel, group), [sds((width, 3 * GROUP), BF16...  31.6 us
    pallas_call x2, Pallas kernels, rows_product(): call(kernel, sds((total, wide), BF16), grid=(steps,), in_specs=[pl.BlockS...  24.7 us
    ppermute x19, waiting for transfers between devices, swap(): return lax.ppermute(value, 'shard', [(i, i ^ mask) for i in range(size)])  22.6 us
    pallas_call x1, Pallas kernels, front(): call(functools.partial(front_kernel, blocks, experts), [sds((seq, width),...  22.5 us
    all_to_all x4, starting transfers between devices, exchange(): lax.all_to_all(value.reshape(size, slots // size, wide), 'shard', split_a...  21.4 us
    ppermute x19, starting transfers between devices, swap(): return lax.ppermute(value, 'shard', [(i, i ^ mask) for i in range(size)])  15.1 us
  transfers between devices with their start and end apart: 34, of which 18 were waited for; matrix products, arithmetic and copies ran while one was open for 7% of the time, Pallas kernels for 41%

profile of v2, /device:TPU:4, one launch (start us, length us, event | category | flops | bytes accessed | tf_op | source)
XLA Modules:
  0.0 374.6 jit_solution(18225829537596217813)
XLA Ops:
  9.5 1.3 concatenate.18.refs_0_
  10.9 1.5 collective-permute-start.1
  12.5 1.9 collective-permute-start.3
  15.2 1.2 slice.46
  16.5 1.5 copy.37.seg_col
  18.1 1.3 scatter.4.bias_ref
  19.4 1.3 pad_add_fusion
  20.7 11.6 %prep.1 = (f32[12,512,512]{2,1,0:T(8,128)}, s32[8,512]{1,0:T(8,128)}, f32[512,128]{1,0:T(8,128)}, bf16[1536,896]{1,0:T(8,128)(2,1)}) custom-call(s32[2,512]{1,0:T(2,128)} %bitcast.112, s32[1,512]{1,0:T(1,128)} %bitcast.103, s32[512,1]{1,0:T(8,128)} %copy.37.seg_col, s32[1,512]{1,0:T(1,128)} %bitcast.98, f32[16,32]{1,0:T(8,128)} %scatter.4.bias_ref, ...), custom_call_target="tpu_custom_call" | custom-call | flops 1207959552 | bytes 14155776 | tf_op jit(solution)/shard_map/prep/pallas_call | solution.py:126
  32.3 7.8 %collective-permute-done.2.refs_2_ = bf16[96,3200]{1,0:T(8,128)(2,1)S(1)} collective-permute-done((bf16[96,3200]{1,0:T(8,128)(2,1)S(1)}, bf16[96,3200]{1,0:T(8,128)(2,1)S(1)}, u32[]{:S(2)}, u32[]{:S(2)}) %collective-permute-start.2) | collective-permute-done | bytes 614432 | tf_op jit(solution)/shard_map/ppermute | solution.py:668
  40.1 1.1 collective-permute-done.3.refs_4_
  42.0 4.4 %all-to-all-start = ((bf16[8,192,896]{2,1,0:T(8,128)(2,1)}), bf16[8,192,896]{2,1,0:T(8,128)(2,1)S(1)}, u32[]{:S(2)}, u32[]{:S(2)}) async-start(bf16[8,192,896]{2,1,0:T(8,128)(2,1)} %bitcast.88), calls=%async_computation | async-start | bytes 5505024 | tf_op jit(solution)/shard_map/all_to_all | solution.py:792
  47.1 1.7 collective-permute-done.4.refs_3_
  48.8 1.0 collective-permute-done.5.refs_5_
  50.7 22.5 %front.1 = (bf16[512,768]{1,0:T(8,128)(2,1)}, bf16[512,768]{1,0:T(8,128)(2,1)}, bf16[512,768]{1,0:T(8,128)(2,1)}, f32[512,128]{1,0:T(8,128)}, bf16[512,768]{1,0:...) custom-call(s32[1]{0:T(128)} %bitcast.me_ref.refs_0_, ...), custom_call_target="tpu_custom_call" | custom-call | flops 5234491392 | bytes 30000000 | tf_op jit(solution)/shard_map/front/pallas_call | solution.py:234
  73.2 5.4 %all-to-all-done = bf16[8,192,896]{2,1,0:T(8,128)(2,1)S(1)} async-done(((bf16[8,192,896]{2,1,0:T(8,128)(2,1)}), bf16[8,192,896]{2,1,0:T(8,128)(2,1)S(1)}, u32[]{:S(2)}, u32[]{:S(2)}) %all-to-all-start) | async-done | bytes 2752544 | tf_op jit(solution)/shard_map/all_to_all | solution.py:792
  78.6 1.5 copy-done.1
  80.1 5.8 %all-to-all-start.1 = ((bf16[8,192,768]{2,1,0:T(8,128)(2,1)}), bf16[8,192,768]{2,1,0:T(8,128)(2,1)}, u32[]{:S(2)}, u32[]{:S(2)}) async-start(bf16[8,192,768]{2,1,0:T(8,128)(2,1)} %bitcast.93), calls=%async_computation.1 | async-start | bytes 4718592 | tf_op jit(solution)/shard_map/all_to_all | solution.py:792
  86.3 4.8 %assemble.1 = (bf16[768,2304]{1,0:T(8,128)(2,1)}, bf16[768,768]{1,0:T(8,128)(2,1)}) custom-call(s32[1]{0:T(128)} %bitcast.me_ref.refs_0_, bf16[96,3200]{1,0:T(8,128)(2,1)} %copy-done.2, bf16[96,3200]{1,0:T(8,128)(2,1)} %copy-done.6, bf16[96,3200]{1,0:T(8,128)(2,1)} %copy-done.8, bf16[96,3200]{1,0:T(8,128)(2,1)} %copy-done.10, bf16[96,3200]{1,0:T(8,128)(2,1)} %copy-done.9, ...), custom_call_target="tpu_custom_call" | custom-call | tf_op jit(solution)/shard_map/assemble/pallas_call | solution.py:276
  91.1 22.9 %all-to-all-done.1 = bf16[8,192,768]{2,1,0:T(8,128)(2,1)} async-done(((bf16[8,192,768]{2,1,0:T(8,128)(2,1)}), bf16[8,192,768]{2,1,0:T(8,128)(2,1)}, u32[]{:S(2)}, u32[]{:S(2)}) %all-to-all-start.1) | async-done | bytes 2359328 | tf_op jit(solution)/shard_map/all_to_all | solution.py:792
  113.9 22.9 %experts.2 = (bf16[1536,3072]{1,0:T(8,128)(2,1)}, bf16[1536,3072]{1,0:T(8,128)(2,1)}, f32[1536,128]{1,0:T(8,128)}, bf16[4,1,384,1024]{3,2,1,0:T(8,128)(2,1)}, bf...) custom-call(s32[1]{0:T(128)} %bitcast.me_ref.refs_0_, ...), custom_call_target="tpu_custom_call" | custom-call | flops 9663676416 | bytes 20000000 | tf_op jit(solution)/shard_map/experts/pallas_call | solution.py:388
  136.9 35.2 %experts.3 = (bf16[1536,3072]{1,0:T(8,128)(2,1)}, bf16[1536,3072]{1,0:T(8,128)(2,1)}, f32[1536,128]{1,0:T(8,128)}, bf16[4,2,384,1024]{3,2,1,0:T(8,128)(2,1)}) custom-call(bf16[1536,768]{1,0:T(8,128)(2,1)} %bitcast.11.refs_1_.refs_0_, bf16[1536,768]{1,0:T(8,128)(2,1)} %get-tuple-element.114.refs_1_, ...), custom_call_target="tpu_custom_call", output_to_operand_aliasing={{0}: (6, {}), {1}: (7, {})} | custom-call | flops 19327352832 | bytes 20000000 | tf_op jit(solution)/shard_map/experts/pallas_call | solution.py:388
  172.1 12.7 %expert_rows_back.1 = bf16[1536,896]{1,0:T(8,128)(2,1)} custom-call(bf16[1536,3072]{1,0:T(8,128)(2,1)} %get-tuple-element.119.a_ref, bf16[768,3072]{1,0:T(8,128)(2,1)} %bitcast.108, f32[1536,128]{1,0:T(8,128)} %get-tuple-element.120.refs_0_, f32[1536,128]{1,0:T(8,128)} %get-tuple-element.121.refs_1_), custom_call_target="tpu_custom_call" | custom-call | flops 8455716864 | bytes 17694720 | tf_op jit(solution)/shard_map/expert_rows_back/pallas_call | solution.py:423
  184.8 5.2 %all-to-all-start.2 = ((bf16[8,192,896]{2,1,0:T(8,128)(2,1)}), bf16[8,192,896]{2,1,0:T(8,128)(2,1)S(1)}, u32[]{:S(2)}, u32[]{:S(2)}) async-start(bf16[8,192,896]{2,1,0:T(8,128)(2,1)} %bitcast.89), calls=%async_computation.2 | async-start | bytes 5505024 | tf_op jit(solution)/shard_map/all_to_all | solution.py:792
  190.0 7.6 %reduce-scatter.3.cloned.1.call-done = bf16[384,1024]{1,0:T(8,128)(2,1)} async-done(((bf16[1536,1024]{1,0:T(8,128)(2,1)}), bf16[384,1024]{1,0:T(8,128)(2,1)}) %reduce-scatter.3.cloned.1.call-update) | async-done | bytes 786448 | tf_op jit(solution)/shard_map/reduce_scatter | solution.py:808
  197.6 12.0 %expert_rows_out.1 = bf16[1536,768]{1,0:T(8,128)(2,1)} custom-call(bf16[1536,3072]{1,0:T(8,128)(2,1)} %get-tuple-element.124.a_ref, bf16[3072,768]{1,0:T(8,128)(2,1)} %bitcast.111), custom_call_target="tpu_custom_call" | custom-call | flops 7247757312 | bytes 16515072 | tf_op jit(solution)/shard_map/expert_rows_out/pallas_call | solution.py:423
  209.7 12.5 %all-to-all-done.2 = bf16[8,192,896]{2,1,0:T(8,128)(2,1)S(1)} async-done(((bf16[8,192,896]{2,1,0:T(8,128)(2,1)}), bf16[8,192,896]{2,1,0:T(8,128)(2,1)S(1)}, u32[]{:S(2)}, u32[]{:S(2)}) %all-to-all-start.2) | async-done | bytes 2752544 | tf_op jit(solution)/shard_map/all_to_all | solution.py:792
  222.2 1.5 copy-done
  223.7 10.7 %token_side.1 = (f32[512,768]{1,0:T(8,128)}, bf16[512,768]{1,0:T(8,128)(2,1)}, bf16[768,896]{1,0:T(8,128)(2,1)}) custom-call(bf16[1536,896]{1,0:T(8,128)(2,1)} %bitcast.79, f32[512,128]{1,0:T(8,128)} %get-tuple-element.126.slot_ref, f32[512,768]{1,0:T(8,128)} %get-tuple-element.127.res_ref, f32[512,128]{1,0:T(8,128)} %get-tuple-element.128.logit_ref, ...), custom_call_target="tpu_custom_call" | custom-call | flops 2415919104 | bytes 12000000 | tf_op jit(solution)/shard_map/token_side/pallas_call | solution.py:514
  234.4 1.2 dynamic-slice_bitcast_fusion.2
  235.7 6.1 %all-to-all-start.3 = ((bf16[8,192,768]{2,1,0:T(8,128)(2,1)}), bf16[8,192,768]{2,1,0:T(8,128)(2,1)}, u32[]{:S(2)}, u32[]{:S(2)}) async-start(bf16[8,192,768]{2,1,0:T(8,128)(2,1)} %bitcast.92), calls=%async_computation.4 | async-start | bytes 4718592 | tf_op jit(solution)/shard_map/all_to_all | solution.py:792
  241.8 10.2 %tail.3 = (bf16[768,768]{1,0:T(8,128)(2,1)}, f32[512,768]{1,0:T(8,128)}, f32[32,512]{1,0:T(8,128)}) custom-call(f32[12,512,512]{2,1,0:T(8,128)} %get-tuple-element.98.table_ref.refs_0_, bf16[512,768]{1,0:T(8,128)(2,1)} %get-tuple-element.138.refs_1_, bf16[512,768]{1,0:T(8,128)(2,1)} %get-tuple-element.139.refs_2_, ...), custom_call_target="tpu_custom_call" | custom-call | flops 2617245696 | bytes 10000000 | tf_op jit(solution)/shard_map/tail/pallas_call | solution.py:609
  252.2 10.7 %tail.4 = (bf16[768,768]{1,0:T(8,128)(2,1)}, f32[512,768]{1,0:T(8,128)}, f32[32,512]{1,0:T(8,128)}) custom-call(f32[12,512,512]{2,1,0:T(8,128)} %get-tuple-element.98.table_ref.refs_0_, bf16[512,768]{1,0:T(8,128)(2,1)} %get-tuple-element.138.refs_1_, bf16[512,768]{1,0:T(8,128)(2,1)} %get-tuple-element.139.refs_2_, ...), custom_call_target="tpu_custom_call" | custom-call | flops 2617245696 | bytes 10000000 | tf_op jit(solution)/shard_map/tail/pallas_call | solution.py:609
  262.9 1.8 pad_maximum_fusion
  264.6 1.1 dynamic-slice_bitcast_fusion
  267.1 2.6 collective-permute-start.8
  270.2 3.4 finish.2
  273.6 3.6 collective-permute-done.10
  277.3 1.3 collective-permute-done.9
  278.6 1.7 fusion.11
  280.3 1.5 fusion
  281.9 4.4 %collective-permute-start.25 = (bf16[96,896]{1,0:T(8,128)(2,1)}, bf16[96,896]{1,0:T(8,128)(2,1)}, u32[]{:S(2)}, u32[]{:S(2)}) collective-permute-start(bf16[96,896]{1,0:T(8,128)(2,1)} %fusion.11), channel_id=1, source_target_pairs={{0,8},{24,16},{1,9},{25,17},{2,10},{26,18},{3,11},{27,19},{4,12},{... | collective-permute-start | bytes 516104 | tf_op jit(solution)/shard_map/ppermute | solution.py:686
  287.1 1.4 collective-permute-start.12
  288.9 1.7 collective-permute-start.14
  290.6 10.7 %tail.5 = (bf16[768,768]{1,0:T(8,128)(2,1)}, f32[512,768]{1,0:T(8,128)}, f32[32,512]{1,0:T(8,128)}) custom-call(f32[12,512,512]{2,1,0:T(8,128)} %get-tuple-element.98.table_ref.refs_0_, bf16[512,768]{1,0:T(8,128)(2,1)} %get-tuple-element.138.refs_1_, bf16[512,768]{1,0:T(8,128)(2,1)} %get-tuple-element.139.refs_2_, ...), custom_call_target="tpu_custom_call" | custom-call | flops 2617245696 | bytes 10000000 | tf_op jit(solution)/shard_map/tail/pallas_call | solution.py:609
  301.4 5.2 %last.1 = (bf16[512,768]{1,0:T(8,128)(2,1)}, bf16[768,128]{1,0:T(8,128)(2,1)}) custom-call(bf16[512,768]{1,0:T(8,128)(2,1)} %tokens_ref.3, f32[512,768]{1,0:T(8,128)} %get-tuple-element.148.gres_ref, f32[512,768]{1,0:T(8,128)} %get-tuple-element.151.acc_ref, f32[128,768]{1,0:T(8,128)} %get-tuple-element.132.small_t_ref, s32[1,512]{1,0:T(1,128)} %bitcast.99, ...), custom_call_target="tpu_custom_call" | custom-call | bytes 5000000 | tf_op jit(solution)/shard_map/last/pallas_call | solution.py:656
  306.6 1.0 pad_maximum_fusion.1
  308.5 5.8 %output_rows.1 = bf16[512,768]{1,0:T(8,128)(2,1)} custom-call(bf16[1536,768]{1,0:T(8,128)(2,1)} %bitcast.26.ret_ref, f32[512,128]{1,0:T(8,128)} %get-tuple-element.126.slot_ref, f32[512,768]{1,0:T(8,128)} %get-tuple-element.127.res_ref, f32[512,128]{1,0:T(8,128)} %get-tuple-element.128.logit_ref), custom_call_target="tpu_custom_call" | custom-call | flops 2415919104 | bytes 6000000 | tf_op jit(solution)/shard_map/output_rows/pallas_call | solution.py:472
  316.0 1.3 fusion.5
  317.3 3.6 collective-permute-start.15
  321.0 1.3 collective-permute-start.27
  322.5 1.5 collective-permute-start.19
  324.4 1.7 collective-permute-start.21
  326.1 1.3 collective-permute-done.15
  328.1 2.7 collective-permute-done.19
  330.8 1.3 collective-permute-done.20
  332.1 1.2 collective-permute-done.21
  333.4 4.3 %collective-permute-start.22 = (bf16[96,896]{1,0:T(8,128)(2,1)S(1)}, bf16[96,896]{1,0:T(8,128)(2,1)S(1)}, u32[]{:S(2)}, u32[]{:S(2)}) collective-permute-start(bf16[96,896]{1,0:T(8,128)(2,1)S(1)} %fusion.8), channel_id=1, source_target_pairs={{0,8},{24,16},{1,9},{25,17},{2,10},{26,18},{3,11},{27,19},{4,12},{... | collective-permute-start | bytes 516104 | tf_op jit(solution)/shard_map/ppermute | solution.py:686
  339.1 2.3 collective-permute-done.22
  342.2 1.3 collective-permute-start.17
  344.3 1.3 collective-permute-start.24
  345.6 10.3 %collective-permute-done.17 = bf16[96,1536]{1,0:T(8,128)(2,1)S(1)} collective-permute-done((bf16[96,1536]{1,0:T(8,128)(2,1)S(1)}, bf16[96,1536]{1,0:T(8,128)(2,1)S(1)}, u32[]{:S(2)}, u32[]{:S(2)}) %collective-permute-start.17) | collective-permute-done | bytes 294944 | tf_op jit(solution)/shard_map/ppermute | solution.py:694
  355.9 1.8 collective-permute-done.24
  358.7 1.5 reshape.127
  361.5 5.7 %finish.3 = (f32[192,3072]{1,0:T(8,128)}, f32[768,768]{1,0:T(8,128)}) custom-call(bf16[2,384,1024]{2,1,0:T(8,128)(2,1)} %bitcast.94, f32[192,3072]{1,0:T(8,128)} %get-tuple-element.162.refs_0_, f32[768,768]{1,0:T(8,128)} %get-tuple-element.163.refs_1_), custom_call_target="tpu_custom_call", output_to_operand_aliasing={{0}: (1, {}), {1}: (2, {})} | custom-call | tf_op jit(solution)/shard_map/finish/pallas_call | solution.py:726
  (89 shorter events, 19.0 us)
Async XLA Ops:
  10.8 21.5 %copy-start.2 = (bf16[96,3200]{1,0:T(8,128)(2,1)}, bf16[96,3200]{1,0:T(8,128)(2,1)S(1)}, u32[]{:S(2)}) copy-start(bf16[96,3200]{1,0:T(8,128)(2,1)S(1)} %concatenate.18.refs_0_) | copy-start | bytes 1843204
  10.8 21.4 %collective-permute-start = (bf16[96,3200]{1,0:T(8,128)(2,1)S(1)}, bf16[96,3200]{1,0:T(8,128)(2,1)S(1)}, u32[]{:S(2)}, u32[]{:S(2)}) collective-permute-start(bf16[96,3200]{1,0:T(8,128)(2,1)S(1)} %concatenate.18.refs_0_), channel_id=1, source_target_pairs={{0,1},{1,0},{2,3},{3,2},{4,5},{5,4},{6,7},{7,6},{8,9},{9,8},{10,11... | collective-permute-start | bytes 1843208 | tf_op jit(solution)/shard_map/ppermute | solution.py:668
  10.9 21.4 %collective-permute-start.1 = (bf16[96,3200]{1,0:T(8,128)(2,1)S(1)}, bf16[96,3200]{1,0:T(8,128)(2,1)S(1)}, u32[]{:S(2)}, u32[]{:S(2)}) collective-permute-start(bf16[96,3200]{1,0:T(8,128)(2,1)S(1)} %concatenate.18.refs_0_), channel_id=1, source_target_pairs={{0,6},{1,7},{2,4},{3,5},{4,2},{5,3},{6,0},{7,1},{8,14},{9,15},{10,... | collective-permute-start | bytes 1843208 | tf_op jit(solution)/shard_map/ppermute | solution.py:668
  12.4 27.7 %collective-permute-start.2 = (bf16[96,3200]{1,0:T(8,128)(2,1)S(1)}, bf16[96,3200]{1,0:T(8,128)(2,1)S(1)}, u32[]{:S(2)}, u32[]{:S(2)}) collective-permute-start(bf16[96,3200]{1,0:T(8,128)(2,1)S(1)} %concatenate.18.refs_0_), channel_id=1, source_target_pairs={{0,2},{1,3},{2,0},{3,1},{4,6},{5,7},{6,4},{7,5},{8,10},{9,11},{10,... | collective-permute-start | bytes 1843208 | tf_op jit(solution)/shard_map/ppermute | solution.py:668
  12.5 28.7 %collective-permute-start.3 = (bf16[96,3200]{1,0:T(8,128)(2,1)S(1)}, bf16[96,3200]{1,0:T(8,128)(2,1)S(1)}, u32[]{:S(2)}, u32[]{:S(2)}) collective-permute-start(bf16[96,3200]{1,0:T(8,128)(2,1)S(1)} %concatenate.18.refs_0_), channel_id=1, source_target_pairs={{0,4},{1,5},{2,6},{3,7},{4,0},{5,1},{6,2},{7,3},{8,12},{9,13},{10,... | collective-permute-start | bytes 1843208 | tf_op jit(solution)/shard_map/ppermute | solution.py:668
  32.2 9.0 %copy-start.6 = (bf16[96,3200]{1,0:T(8,128)(2,1)}, bf16[96,3200]{1,0:T(8,128)(2,1)S(1)}, u32[]{:S(2)}) copy-start(bf16[96,3200]{1,0:T(8,128)(2,1)S(1)} %collective-permute-done.refs_1_) | copy-start | bytes 1843204
  32.3 9.0 %copy-start.7 = (bf16[96,3200]{1,0:T(8,128)(2,1)}, bf16[96,3200]{1,0:T(8,128)(2,1)S(1)}, u32[]{:S(2)}) copy-start(bf16[96,3200]{1,0:T(8,128)(2,1)S(1)} %collective-permute-done.1.refs_6_) | copy-start | bytes 1843204
  40.1 1.1 copy-start.8
  41.2 0.8 copy-start.9
  42.0 36.6 %all-to-all-start = ((bf16[8,192,896]{2,1,0:T(8,128)(2,1)}), bf16[8,192,896]{2,1,0:T(8,128)(2,1)S(1)}, u32[]{:S(2)}, u32[]{:S(2)}) async-start(bf16[8,192,896]{2,1,0:T(8,128)(2,1)} %bitcast.88), calls=%async_computation | async-start | bytes 5505024 | tf_op jit(solution)/shard_map/all_to_all | solution.py:792
  46.4 2.4 collective-permute-start.4
  46.5 3.2 collective-permute-start.5
  46.9 3.8 %collective-permute-start.6 = (bf16[96,3200]{1,0:T(8,128)(2,1)}, bf16[96,3200]{1,0:T(8,128)(2,1)}, u32[]{:S(2)}, u32[]{:S(2)}) collective-permute-start(bf16[96,3200]{1,0:T(8,128)(2,1)} %copy-done.7), channel_id=1, source_target_pairs={{0,1},{1,0},{2,3},{3,2},{4,5},{5,4},{6,7},{7,6},{8,9},{9,8},{10,11... | collective-permute-start | bytes 1843208 | tf_op jit(solution)/shard_map/ppermute | solution.py:668
  48.8 1.9 copy-start.10
  78.6 1.5 copy-start.1
  80.1 33.8 %all-to-all-start.1 = ((bf16[8,192,768]{2,1,0:T(8,128)(2,1)}), bf16[8,192,768]{2,1,0:T(8,128)(2,1)}, u32[]{:S(2)}, u32[]{:S(2)}) async-start(bf16[8,192,768]{2,1,0:T(8,128)(2,1)} %bitcast.93), calls=%async_computation.1 | async-start | bytes 4718592 | tf_op jit(solution)/shard_map/all_to_all | solution.py:792
  85.9 111.8 %reduce-scatter.3.cloned.1.call-start = ((), (), s32[]{:S(2)}) async-start(), calls=%async_computation.6 | async-start | bytes 3932160 | tf_op jit(solution)/shard_map/reduce_scatter | solution.py:808
  136.9 224.7 %reduce-scatter.5.cloned.1.call-start = ((), (), s32[]{:S(2)}) async-start(), calls=%async_computation.7 | async-start | bytes 7864320 | tf_op jit(solution)/shard_map/reduce_scatter | solution.py:808
  184.8 37.4 %all-to-all-start.2 = ((bf16[8,192,896]{2,1,0:T(8,128)(2,1)}), bf16[8,192,896]{2,1,0:T(8,128)(2,1)S(1)}, u32[]{:S(2)}, u32[]{:S(2)}) async-start(bf16[8,192,896]{2,1,0:T(8,128)(2,1)} %bitcast.89), calls=%async_computation.2 | async-start | bytes 5505024 | tf_op jit(solution)/shard_map/all_to_all | solution.py:792
  222.2 1.5 copy-start
  235.6 16.4 %collective-permute-start.7 = (bf16[4,96,896]{2,1,0:T(8,128)(2,1)S(1)}, bf16[4,96,896]{2,1,0:T(8,128)(2,1)S(1)}, u32[]{:S(2)}, u32[]{:S(2)}) collective-permute-start(bf16[4,96,896]{2,1,0:T(8,128)(2,1)S(1)} %dynamic-slice_bitcast_fusion.2), channel_id=1, source_target_pairs={{0,1},{1,0},{2,3},{3,2},{4,5},{5,4},{6,7},{7,6},{8,9},{9,8},{10,11... | collective-permute-start | bytes 2064392 | tf_op jit(solution)/shard_map/ppermute | solution.py:668
  235.7 46.2 %all-to-all-start.3 = ((bf16[8,192,768]{2,1,0:T(8,128)(2,1)}), bf16[8,192,768]{2,1,0:T(8,128)(2,1)}, u32[]{:S(2)}, u32[]{:S(2)}) async-start(bf16[8,192,768]{2,1,0:T(8,128)(2,1)} %bitcast.92), calls=%async_computation.4 | async-start | bytes 4718592 | tf_op jit(solution)/shard_map/all_to_all | solution.py:792
  241.8 10.2 %copy-start.3 = (bf16[768,896]{1,0:T(8,128)(2,1)S(1)}, bf16[768,896]{1,0:T(8,128)(2,1)}, u32[]{:S(2)}) copy-start(bf16[768,896]{1,0:T(8,128)(2,1)} %get-tuple-element.134) | copy-start | bytes 4128772
  265.8 14.5 %collective-permute-start.11 = (bf16[4,96,1536]{2,1,0:T(8,128)(2,1)}, bf16[4,96,1536]{2,1,0:T(8,128)(2,1)}, u32[]{:S(2)}, u32[]{:S(2)}) collective-permute-start(bf16[4,96,1536]{2,1,0:T(8,128)(2,1)} %dynamic-slice_bitcast_fusion), channel_id=1, source_target_pairs={{0,1},{1,0},{2,3},{3,2},{4,5},{5,4},{6,7},{7,6},{8,9},{9,8},{10,11... | collective-permute-start | bytes 3538952 | tf_op jit(solution)/shard_map/ppermute | solution.py:668
  266.7 10.5 %collective-permute-start.10 = (bf16[96,896]{1,0:T(8,128)(2,1)}, bf16[96,896]{1,0:T(8,128)(2,1)S(1)}, u32[]{:S(2)}, u32[]{:S(2)}) collective-permute-start(bf16[96,896]{1,0:T(8,128)(2,1)} %get-tuple-element.193), channel_id=1, source_target_pairs={{0,4},{1,5},{2,6},{3,7},{4,0},{5,1},{6,2},{7,3},{8,12},{9,13},{10,... | collective-permute-start | bytes 516104 | tf_op jit(solution)/shard_map/ppermute | solution.py:668
  267.1 10.2 %collective-permute-start.8 = (bf16[96,896]{1,0:T(8,128)(2,1)}, bf16[96,896]{1,0:T(8,128)(2,1)S(1)}, u32[]{:S(2)}, u32[]{:S(2)}) collective-permute-start(bf16[96,896]{1,0:T(8,128)(2,1)} %get-tuple-element.192), channel_id=1, source_target_pairs={{0,6},{1,7},{2,4},{3,5},{4,2},{5,3},{6,0},{7,1},{8,14},{9,15},{10,... | collective-permute-start | bytes 516104 | tf_op jit(solution)/shard_map/ppermute | solution.py:668
  269.7 8.9 %collective-permute-start.9 = (bf16[96,896]{1,0:T(8,128)(2,1)}, bf16[96,896]{1,0:T(8,128)(2,1)}, u32[]{:S(2)}, u32[]{:S(2)}) collective-permute-start(bf16[96,896]{1,0:T(8,128)(2,1)} %get-tuple-element.194), channel_id=1, source_target_pairs={{0,2},{1,3},{2,0},{3,1},{4,6},{5,7},{6,4},{7,5},{8,10},{9,11},{10,... | collective-permute-start | bytes 516104 | tf_op jit(solution)/shard_map/ppermute | solution.py:668
  281.9 32.5 %collective-permute-start.25 = (bf16[96,896]{1,0:T(8,128)(2,1)}, bf16[96,896]{1,0:T(8,128)(2,1)}, u32[]{:S(2)}, u32[]{:S(2)}) collective-permute-start(bf16[96,896]{1,0:T(8,128)(2,1)} %fusion.11), channel_id=1, source_target_pairs={{0,8},{24,16},{1,9},{25,17},{2,10},{26,18},{3,11},{27,19},{4,12},{... | collective-permute-start | bytes 516104 | tf_op jit(solution)/shard_map/ppermute | solution.py:686
  287.1 28.8 %collective-permute-start.12 = (bf16[96,1536]{1,0:T(8,128)(2,1)}, bf16[96,1536]{1,0:T(8,128)(2,1)}, u32[]{:S(2)}, u32[]{:S(2)}) collective-permute-start(bf16[96,1536]{1,0:T(8,128)(2,1)} %get-tuple-element.186), channel_id=1, source_target_pairs={{0,6},{1,7},{2,4},{3,5},{4,2},{5,3},{6,0},{7,1},{8,14},{9,15},{10,... | collective-permute-start | bytes 884744 | tf_op jit(solution)/shard_map/ppermute | solution.py:668
  288.6 27.4 %collective-permute-start.13 = (bf16[96,1536]{1,0:T(8,128)(2,1)}, bf16[96,1536]{1,0:T(8,128)(2,1)}, u32[]{:S(2)}, u32[]{:S(2)}) collective-permute-start(bf16[96,1536]{1,0:T(8,128)(2,1)} %get-tuple-element.188), channel_id=1, source_target_pairs={{0,2},{1,3},{2,0},{3,1},{4,6},{5,7},{6,4},{7,5},{8,10},{9,11},{10,... | collective-permute-start | bytes 884744 | tf_op jit(solution)/shard_map/ppermute | solution.py:668
  288.9 27.1 %collective-permute-start.14 = (bf16[96,1536]{1,0:T(8,128)(2,1)S(1)}, bf16[96,1536]{1,0:T(8,128)(2,1)}, u32[]{:S(2)}, u32[]{:S(2)}) collective-permute-start(bf16[96,1536]{1,0:T(8,128)(2,1)S(1)} %get-tuple-element.187), channel_id=1, source_target_pairs={{0,4},{1,5},{2,6},{3,7},{4,0},{5,1},{6,2},{7,3},{8,12},{9,13},{10,... | collective-permute-start | bytes 884744 | tf_op jit(solution)/shard_map/ppermute | solution.py:668
  301.4 5.2 %copy-start.4 = (bf16[768,768]{1,0:T(8,128)(2,1)S(1)}, bf16[768,768]{1,0:T(8,128)(2,1)}, u32[]{:S(2)}) copy-start(bf16[768,768]{1,0:T(8,128)(2,1)} %get-tuple-element.157) | copy-start | bytes 3538948
  308.5 5.8 %copy-start.5 = (bf16[96,896]{1,0:T(8,128)(2,1)S(1)}, bf16[96,896]{1,0:T(8,128)(2,1)}, u32[]{:S(2)}) copy-start(bf16[96,896]{1,0:T(8,128)(2,1)} %fusion.11) | copy-start | bytes 516100
  308.5 13.7 %collective-permute-start.18 = (bf16[4,96,896]{2,1,0:T(8,128)(2,1)}, bf16[4,96,896]{2,1,0:T(8,128)(2,1)S(1)}, u32[]{:S(2)}, u32[]{:S(2)}) collective-permute-start(bf16[4,96,896]{2,1,0:T(8,128)(2,1)} %dynamic-slice_bitcast_fusion.1), channel_id=1, source_target_pairs={{0,1},{1,0},{2,3},{3,2},{4,5},{5,4},{6,7},{7,6},{8,9},{9,8},{10,11... | collective-permute-start | bytes 2064392 | tf_op jit(solution)/shard_map/ppermute | solution.py:668
  315.3 5.6 %collective-permute-start.26 = (bf16[96,896]{1,0:T(8,128)(2,1)S(1)}, bf16[96,896]{1,0:T(8,128)(2,1)S(1)}, u32[]{:S(2)}, u32[]{:S(2)}) collective-permute-start(bf16[96,896]{1,0:T(8,128)(2,1)S(1)} %add_convert_fusion.3), channel_id=1, source_target_pairs={{8,16},{16,8},{9,17},{17,9},{10,18},{18,10},{11,19},{19,11},{12,20... | collective-permute-start | bytes 516104 | tf_op jit(solution)/shard_map/ppermute | solution.py:690
  317.3 10.1 %collective-permute-start.15 = (bf16[96,1536]{1,0:T(8,128)(2,1)S(1)}, bf16[96,1536]{1,0:T(8,128)(2,1)S(1)}, u32[]{:S(2)}, u32[]{:S(2)}) collective-permute-start(bf16[96,1536]{1,0:T(8,128)(2,1)S(1)} %fusion.5), channel_id=1, source_target_pairs={{0,8},{24,16},{1,9},{25,17},{2,10},{26,18},{3,11},{27,19},{4,12},{... | collective-permute-start | bytes 884744 | tf_op jit(solution)/shard_map/ppermute | solution.py:686
  321.0 16.7 %collective-permute-start.27 = (bf16[96,896]{1,0:T(8,128)(2,1)S(1)}, bf16[96,896]{1,0:T(8,128)(2,1)S(1)}, u32[]{:S(2)}, u32[]{:S(2)}) collective-permute-start(bf16[96,896]{1,0:T(8,128)(2,1)S(1)} %add_convert_fusion.2), channel_id=1, source_target_pairs={{8,0},{16,24},{9,1},{17,25},{10,2},{18,26},{11,3},{19,27},{12,4},{... | collective-permute-start | bytes 516104 | tf_op jit(solution)/shard_map/ppermute | solution.py:694
  322.5 8.3 %collective-permute-start.19 = (bf16[96,896]{1,0:T(8,128)(2,1)S(1)}, bf16[96,896]{1,0:T(8,128)(2,1)S(1)}, u32[]{:S(2)}, u32[]{:S(2)}) collective-permute-start(bf16[96,896]{1,0:T(8,128)(2,1)S(1)} %get-tuple-element.189), channel_id=1, source_target_pairs={{0,6},{1,7},{2,4},{3,5},{4,2},{5,3},{6,0},{7,1},{8,14},{9,15},{10,... | collective-permute-start | bytes 516104 | tf_op jit(solution)/shard_map/ppermute | solution.py:668
  324.1 8.0 %collective-permute-start.20 = (bf16[96,896]{1,0:T(8,128)(2,1)S(1)}, bf16[96,896]{1,0:T(8,128)(2,1)S(1)}, u32[]{:S(2)}, u32[]{:S(2)}) collective-permute-start(bf16[96,896]{1,0:T(8,128)(2,1)S(1)} %get-tuple-element.191), channel_id=1, source_target_pairs={{0,2},{1,3},{2,0},{3,1},{4,6},{5,7},{6,4},{7,5},{8,10},{9,11},{10,... | collective-permute-start | bytes 516104 | tf_op jit(solution)/shard_map/ppermute | solution.py:668
  324.4 8.9 %collective-permute-start.21 = (bf16[96,896]{1,0:T(8,128)(2,1)S(1)}, bf16[96,896]{1,0:T(8,128)(2,1)S(1)}, u32[]{:S(2)}, u32[]{:S(2)}) collective-permute-start(bf16[96,896]{1,0:T(8,128)(2,1)S(1)} %get-tuple-element.190), channel_id=1, source_target_pairs={{0,4},{1,5},{2,6},{3,7},{4,0},{5,1},{6,2},{7,3},{8,12},{9,13},{10,... | collective-permute-start | bytes 516104 | tf_op jit(solution)/shard_map/ppermute | solution.py:668
  327.5 14.7 %collective-permute-start.16 = (bf16[96,1536]{1,0:T(8,128)(2,1)S(1)}, bf16[96,1536]{1,0:T(8,128)(2,1)S(1)}, u32[]{:S(2)}, u32[]{:S(2)}) collective-permute-start(bf16[96,1536]{1,0:T(8,128)(2,1)S(1)} %add_convert_fusion.1), channel_id=1, source_target_pairs={{8,16},{16,8},{9,17},{17,9},{10,18},{18,10},{11,19},{19,11},{12,20... | collective-permute-start | bytes 884744 | tf_op jit(solution)/shard_map/ppermute | solution.py:690
  333.4 8.1 %collective-permute-start.22 = (bf16[96,896]{1,0:T(8,128)(2,1)S(1)}, bf16[96,896]{1,0:T(8,128)(2,1)S(1)}, u32[]{:S(2)}, u32[]{:S(2)}) collective-permute-start(bf16[96,896]{1,0:T(8,128)(2,1)S(1)} %fusion.8), channel_id=1, source_target_pairs={{0,8},{24,16},{1,9},{25,17},{2,10},{26,18},{3,11},{27,19},{4,12},{... | collective-permute-start | bytes 516104 | tf_op jit(solution)/shard_map/ppermute | solution.py:686
  341.5 2.8 collective-permute-start.23
  342.2 13.7 %collective-permute-start.17 = (bf16[96,1536]{1,0:T(8,128)(2,1)S(1)}, bf16[96,1536]{1,0:T(8,128)(2,1)S(1)}, u32[]{:S(2)}, u32[]{:S(2)}) collective-permute-start(bf16[96,1536]{1,0:T(8,128)(2,1)S(1)} %add_convert_fusion), channel_id=1, source_target_pairs={{8,0},{16,24},{9,1},{17,25},{10,2},{18,26},{11,3},{19,27},{12,4},{... | collective-permute-start | bytes 884744 | tf_op jit(solution)/shard_map/ppermute | solution.py:694
  344.3 13.4 %collective-permute-start.24 = (bf16[96,896]{1,0:T(8,128)(2,1)S(1)}, bf16[96,896]{1,0:T(8,128)(2,1)S(1)}, u32[]{:S(2)}, u32[]{:S(2)}) collective-permute-start(bf16[96,896]{1,0:T(8,128)(2,1)S(1)} %add_convert_fusion.4), channel_id=1, source_target_pairs={{8,0},{16,24},{9,1},{17,25},{10,2},{18,26},{11,3},{19,27},{12,4},{... | collective-permute-start | bytes 516104 | tf_op jit(solution)/shard_map/ppermute | solution.py:694
Sparse Core Ops, SparseCore 0:
  137.0 60.5 reduce-scatter.2
  199.9 112.9 reduce-scatter.4
